TPU v7x, 768 devices: a whole 4x8x12 slice. The times are simulated.
768 devices in a mesh: theta: 96 (over y_lo, z, x), axial: 8 (over y_hi, core).
Axes of the slice: x: 4, y: 8 (y_hi: 4, y_lo: 2; y = y_hi * 2 + y_lo), z: 12, core: 2. Of those that a mesh axis runs over, the one named last changes fastest.
Arguments:
- conserved: float32 [5, 1536, 128, 128], P(None, 'theta', 'axial'), may hold values from -6 to 6
- flux_matrices: float32 [3, 5, 5], replicated, may hold values from -2.5 to 2.5
- slide_weights: float32 [3, 2, 16, 16], replicated, may hold values from -1.5 to 1.5
- rotor_offsets: int32 [3], replicated, may hold values from 0 to 95
Outputs:
- advanced: float32 [5, 1536, 128, 128], P(None, 'theta', 'axial')
All inputs are finite; a program needn't handle non-finite values.
Results may differ from a plain program's by a relative error of at most 0.00005.
Values sent between devices are 32-bit elements; how exact they have to be, the bound alone decides.
No kernel may reach another device: no remote copies, remote signals or barrier semaphores. Data moves between devices by JAX's collectives and lax.ppermute only.
A program may use at most 32 MiB of HBM per device.

v0:
```python
import jax
import jax.numpy as jnp
from jax import lax
from jax.sharding import PartitionSpec as P

time_step = 0.25
viscosity = 0.3


def extended(block, sides, width, periodic):
    for axis, dim in sides:
        count = lax.axis_size(axis)
        forward = [(i, i + 1) for i in range(count - 1)]
        if periodic:
            forward.append((count - 1, 0))
        backward = [(target, source) for source, target in forward]
        low = lax.ppermute(
            lax.slice_in_dim(block, block.shape[dim] - width, None, axis=dim), axis, forward
        )
        high = lax.ppermute(lax.slice_in_dim(block, 0, width, axis=dim), axis, backward)
        block = jnp.concatenate([low, block, high], axis=dim)
    return block


def shifted(shard, axis, by):
    size = lax.axis_size(axis)
    return lax.ppermute(shard, axis, [(i, (i + by) % size) for i in range(size)])


def apply_matrix(matrix, values):
    return jnp.einsum("vw,wtar->vtar", matrix, values, precision=lax.Precision.HIGHEST)


def tendency(current, theta_plus, theta_minus, axial_plus, axial_minus, flux_matrices):
    radial_plus = jnp.concatenate([current[..., 1:], current[..., -1:]], axis=3)
    radial_minus = jnp.concatenate([current[..., :1], current[..., :-1]], axis=3)
    transport = apply_matrix(flux_matrices[0], 0.5 * (theta_plus - theta_minus))
    transport = transport + apply_matrix(flux_matrices[1], 0.5 * (axial_plus - axial_minus))
    transport = transport + apply_matrix(flux_matrices[2], 0.5 * (radial_plus - radial_minus))
    diffusion = (
        theta_plus
        + theta_minus
        + axial_plus
        + axial_minus
        + radial_plus
        + radial_minus
        - 6.0 * current
    )
    return viscosity * diffusion - transport


def gather_rims(current):
    theta_ext = extended(current, (("theta", 1),), 1, True)
    axial_ext = extended(current, (("axial", 2),), 1, False)
    return (theta_ext[:, 0], theta_ext[:, -1], axial_ext[:, :, 0], axial_ext[:, :, -1])


def rotate_faces(lower_face, upper_face, offset):
    sectors = lax.axis_size("theta")
    backward = (sectors - offset) % sectors
    for hop_level in range((sectors - 1).bit_length()):
        distance = 1 << hop_level
        moved = shifted((lower_face, upper_face), "theta", distance)
        lower_face = jnp.where(offset // distance % 2 == 1, moved[0], lower_face)
        upper_face = jnp.where(backward // distance % 2 == 1, moved[1], upper_face)
    return (lower_face, upper_face)


def evaluate(current, section_index, flux_matrices, slide_weights, rotor_offsets):
    left_ghost, right_ghost, lower_ghost, upper_ghost = gather_rims(current)
    turned_lower, turned_upper = rotate_faces(
        lower_ghost, upper_ghost, rotor_offsets[section_index]
    )
    from_rotor = jnp.einsum(
        "cd,vdr->vcr",
        slide_weights[section_index, 0],
        turned_lower,
        precision=lax.Precision.HIGHEST,
    )
    from_stator = jnp.einsum(
        "cd,vdr->vcr",
        slide_weights[section_index, 1],
        turned_upper,
        precision=lax.Precision.HIGHEST,
    )
    block_index = lax.axis_index("axial")
    blocks_count = lax.axis_size("axial")
    lower_ghost = jnp.where(block_index == blocks_count // 2, from_rotor, lower_ghost)
    lower_ghost = jnp.where(block_index == 0, current[:, :, 0], lower_ghost)
    upper_ghost = jnp.where(block_index == blocks_count // 2 - 1, from_stator, upper_ghost)
    upper_ghost = jnp.where(block_index == blocks_count - 1, current[:, :, -1], upper_ghost)
    theta_plus = jnp.concatenate([current[:, 1:], right_ghost[:, None]], axis=1)
    theta_minus = jnp.concatenate([left_ghost[:, None], current[:, :-1]], axis=1)
    axial_plus = jnp.concatenate([current[:, :, 1:], upper_ghost[:, :, None]], axis=2)
    axial_minus = jnp.concatenate([lower_ghost[:, :, None], current[:, :, :-1]], axis=2)
    return tendency(current, theta_plus, theta_minus, axial_plus, axial_minus, flux_matrices)


def local(conserved, flux_matrices, slide_weights, rotor_offsets):
    first = conserved + time_step * evaluate(
        conserved, 0, flux_matrices, slide_weights, rotor_offsets
    )
    second = 0.75 * conserved + 0.25 * (
        first + time_step * evaluate(first, 1, flux_matrices, slide_weights, rotor_offsets)
    )
    third = second + time_step * evaluate(second, 2, flux_matrices, slide_weights, rotor_offsets)
    return 1.0 / 3.0 * conserved + 2.0 / 3.0 * third


def solution(mesh):
    in_specs = (P(None, "theta", "axial", None), P(), P(), P())
    out_specs = P(None, "theta", "axial", None)
    return jax.shard_map(local, mesh=mesh, in_specs=in_specs, out_specs=out_specs, check_vma=False)
```

profile of v0, /device:TPU:48, one launch (start us, length us, event | category | flops | bytes accessed | tf_op | source)
XLA Modules:
  0.0 309.7 jit_solution(2956012091574140467)
XLA Ops:
  1.4 3.5 %collective-permute-start.2 = (f32[5,16,1,128]{3,1,0,2:T(8,128)S(1)}, f32[5,16,1,128]{3,1,0,2:T(8,128)S(1)}, u32[]{:S(2)}, u32[]{:S(2)}) collective-permute-start(f32[5,16,1,128]{3,1,0,2:T(8,128)S(1)} %get-tuple-element.35), channel_id=1, source_target_pairs={{1,0},{2,1},{3,2},{4,3},{5,4},{6,5},{7,6},{9,8},{10,9},{11,10},{12... | collective-permute-start | bytes 122888 | tf_op jit(solution)/shard_map/ppermute | solution.py:20
  4.9 1.9 collective-permute-start.10
  7.5 16.9 %collective-permute-start = (f32[5,1,16,128]{3,1,0,2:T(1,128)}, f32[5,1,16,128]{3,1,0,2:T(1,128)S(1)}, u32[]{:S(2)}, u32[]{:S(2)}) collective-permute-start(f32[5,1,16,128]{3,1,0,2:T(1,128)} %copy.8), channel_id=1, source_target_pairs={{8,0},{16,8},{24,16},{32,24},{40,32},{48,40},{56,48},{64,56},{72,6... | collective-permute-start | bytes 122888 | tf_op jit(solution)/shard_map/ppermute | solution.py:20
  34.4 2.2 fusion.30
  46.6 1.9 collective-permute-start.3
  48.6 1.9 collective-permute-start.11
  51.9 4.8 %collective-permute-done.3 = f32[5,16,128]{2,1,0:T(8,128)S(1)} collective-permute-done((f32[5,16,128]{2,1,0:T(8,128)S(1)}, f32[5,16,128]{2,1,0:T(8,128)S(1)}, u32[]{:S(2)}, u32[]{:S(2)}) %collective-permute-start.3) | collective-permute-done | bytes 40992 | tf_op jit(solution)/shard_map/ppermute | solution.py:27
  58.7 1.9 collective-permute-start.12
  60.6 6.8 %collective-permute-done.4 = f32[5,16,128]{2,1,0:T(8,128)S(1)} collective-permute-done((f32[5,16,128]{2,1,0:T(8,128)S(1)}, f32[5,16,128]{2,1,0:T(8,128)S(1)}, u32[]{:S(2)}, u32[]{:S(2)}) %collective-permute-start.4) | collective-permute-done | bytes 40992 | tf_op jit(solution)/shard_map/ppermute | solution.py:27
  69.4 1.9 collective-permute-start.13
  71.3 4.1 %collective-permute-done.5 = f32[5,16,128]{2,1,0:T(8,128)S(1)} collective-permute-done((f32[5,16,128]{2,1,0:T(8,128)S(1)}, f32[5,16,128]{2,1,0:T(8,128)S(1)}, u32[]{:S(2)}, u32[]{:S(2)}) %collective-permute-start.5) | collective-permute-done | bytes 40992 | tf_op jit(solution)/shard_map/ppermute | solution.py:27
  75.4 2.1 collective-permute-start.6
  78.2 2.1 collective-permute-start.14
  80.2 4.8 %collective-permute-done.6 = f32[5,16,128]{2,1,0:T(8,128)S(1)} collective-permute-done((f32[5,16,128]{2,1,0:T(8,128)S(1)}, f32[5,16,128]{2,1,0:T(8,128)S(1)}, u32[]{:S(2)}, u32[]{:S(2)}) %collective-permute-start.6) | collective-permute-done | bytes 40992 | tf_op jit(solution)/shard_map/ppermute | solution.py:27
  85.1 1.9 collective-permute-start.7
  87.3 6.4 %collective-permute-start.15 = (f32[5,16,128]{2,1,0:T(8,128)S(1)}, f32[5,16,128]{2,1,0:T(8,128)S(1)}, u32[]{:S(2)}, u32[]{:S(2)}) collective-permute-start(f32[5,16,128]{2,1,0:T(8,128)S(1)} %broadcast_select_fusion.27), channel_id=1, source_target_pairs={{0,128},{8,136},{16,144},{24,152},{32,160},{40,168},{48,176},{56,1... | collective-permute-start | bytes 122888 | tf_op jit(solution)/shard_map/ppermute | solution.py:27
  93.7 2.5 collective-permute-done.7
  96.2 2.8 collective-permute-start.8
  99.1 6.5 %collective-permute-start.16 = (f32[5,16,128]{2,1,0:T(8,128)S(1)}, f32[5,16,128]{2,1,0:T(8,128)S(1)}, u32[]{:S(2)}, u32[]{:S(2)}) collective-permute-start(f32[5,16,128]{2,1,0:T(8,128)S(1)} %broadcast_select_fusion.28), channel_id=1, source_target_pairs={{0,256},{8,264},{16,272},{24,280},{32,288},{40,296},{48,304},{56,3... | collective-permute-start | bytes 122888 | tf_op jit(solution)/shard_map/ppermute | solution.py:27
  107.5 3.9 %collective-permute-start.9 = (f32[5,16,128]{2,1,0:T(8,128)S(1)}, f32[5,16,128]{2,1,0:T(8,128)S(1)}, u32[]{:S(2)}, u32[]{:S(2)}) collective-permute-start(f32[5,16,128]{2,1,0:T(8,128)S(1)} %broadcast_select_fusion.35), channel_id=1, source_target_pairs={{0,512},{8,520},{16,528},{24,536},{32,544},{40,552},{48,560},{56,5... | collective-permute-start | bytes 122888 | tf_op jit(solution)/shard_map/ppermute | solution.py:27
  111.4 6.2 %collective-permute-start.17 = (f32[5,16,128]{2,1,0:T(8,128)S(1)}, f32[5,16,128]{2,1,0:T(8,128)S(1)}, u32[]{:S(2)}, u32[]{:S(2)}) collective-permute-start(f32[5,16,128]{2,1,0:T(8,128)S(1)} %broadcast_select_fusion.29), channel_id=1, source_target_pairs={{0,512},{8,520},{16,528},{24,536},{32,544},{40,552},{48,560},{56,5... | collective-permute-start | bytes 122888 | tf_op jit(solution)/shard_map/ppermute | solution.py:27
  117.8 4.0 %collective-permute-done.17 = f32[5,16,128]{2,1,0:T(8,128)S(1)} collective-permute-done((f32[5,16,128]{2,1,0:T(8,128)S(1)}, f32[5,16,128]{2,1,0:T(8,128)S(1)}, u32[]{:S(2)}, u32[]{:S(2)}) %collective-permute-start.17) | collective-permute-done | bytes 40992 | tf_op jit(solution)/shard_map/ppermute | solution.py:27
  123.8 2.0 fusion.45
  126.4 1.9 collective-permute-start.18
  128.4 3.9 %collective-permute-start.19 = (f32[5,1,16,128]{3,1,0,2:T(1,128)S(1)}, f32[5,1,16,128]{3,1,0,2:T(1,128)S(1)}, u32[]{:S(2)}, u32[]{:S(2)}) collective-permute-start(f32[5,1,16,128]{3,1,0,2:T(1,128)S(1)} %get-tuple-element.20), channel_id=1, source_target_pairs={{0,8},{8,16},{16,24},{24,32},{32,40},{40,48},{48,56},{56,64},{64,7... | collective-permute-start | bytes 122888 | tf_op jit(solution)/shard_map/ppermute | solution.py:17
  132.3 1.9 collective-permute-start.20
  134.2 2.6 collective-permute-start.28
  138.5 1.9 collective-permute-start.21
  141.9 1.9 collective-permute-start.29
  143.8 4.8 %collective-permute-done.21 = f32[5,16,128]{2,1,0:T(8,128)S(1)} collective-permute-done((f32[5,16,128]{2,1,0:T(8,128)S(1)}, f32[5,16,128]{2,1,0:T(8,128)S(1)}, u32[]{:S(2)}, u32[]{:S(2)}) %collective-permute-start.21) | collective-permute-done | bytes 40992 | tf_op jit(solution)/shard_map/ppermute | solution.py:27
  154.1 4.9 %collective-permute-done.22 = f32[5,16,128]{2,1,0:T(8,128)S(1)} collective-permute-done((f32[5,16,128]{2,1,0:T(8,128)S(1)}, f32[5,16,128]{2,1,0:T(8,128)S(1)}, u32[]{:S(2)}, u32[]{:S(2)}) %collective-permute-start.22) | collective-permute-done | bytes 40992 | tf_op jit(solution)/shard_map/ppermute | solution.py:27
  164.5 2.5 collective-permute-done.23
  170.7 2.7 collective-permute-start.32
  173.4 2.7 collective-permute-done.24
  176.1 2.8 collective-permute-start.25
  179.6 5.2 %collective-permute-start.33 = (f32[5,16,128]{2,1,0:T(8,128)S(1)}, f32[5,16,128]{2,1,0:T(8,128)S(1)}, u32[]{:S(2)}, u32[]{:S(2)}) collective-permute-start(f32[5,16,128]{2,1,0:T(8,128)S(1)} %broadcast_select_fusion.15), channel_id=1, source_target_pairs={{0,128},{8,136},{16,144},{24,152},{32,160},{40,168},{48,176},{56,1... | collective-permute-start | bytes 122888 | tf_op jit(solution)/shard_map/ppermute | solution.py:27
  184.8 2.5 collective-permute-done.25
  187.3 4.3 %collective-permute-start.26 = (f32[5,16,128]{2,1,0:T(8,128)S(1)}, f32[5,16,128]{2,1,0:T(8,128)S(1)}, u32[]{:S(2)}, u32[]{:S(2)}) collective-permute-start(f32[5,16,128]{2,1,0:T(8,128)S(1)} %broadcast_select_fusion.22), channel_id=1, source_target_pairs={{0,256},{8,264},{16,272},{24,280},{32,288},{40,296},{48,304},{56,3... | collective-permute-start | bytes 122888 | tf_op jit(solution)/shard_map/ppermute | solution.py:27
  191.5 5.1 %collective-permute-start.34 = (f32[5,16,128]{2,1,0:T(8,128)S(1)}, f32[5,16,128]{2,1,0:T(8,128)S(1)}, u32[]{:S(2)}, u32[]{:S(2)}) collective-permute-start(f32[5,16,128]{2,1,0:T(8,128)S(1)} %broadcast_select_fusion.16), channel_id=1, source_target_pairs={{0,256},{8,264},{16,272},{24,280},{32,288},{40,296},{48,304},{56,3... | collective-permute-start | bytes 122888 | tf_op jit(solution)/shard_map/ppermute | solution.py:27
  198.2 5.4 %collective-permute-start.27 = (f32[5,16,128]{2,1,0:T(8,128)S(1)}, f32[5,16,128]{2,1,0:T(8,128)S(1)}, u32[]{:S(2)}, u32[]{:S(2)}) collective-permute-start(f32[5,16,128]{2,1,0:T(8,128)S(1)} %broadcast_select_fusion.23), channel_id=1, source_target_pairs={{0,512},{8,520},{16,528},{24,536},{32,544},{40,552},{48,560},{56,5... | collective-permute-start | bytes 122888 | tf_op jit(solution)/shard_map/ppermute | solution.py:27
  203.6 5.1 %collective-permute-start.35 = (f32[5,16,128]{2,1,0:T(8,128)S(1)}, f32[5,16,128]{2,1,0:T(8,128)S(1)}, u32[]{:S(2)}, u32[]{:S(2)}) collective-permute-start(f32[5,16,128]{2,1,0:T(8,128)S(1)} %broadcast_select_fusion.17), channel_id=1, source_target_pairs={{0,512},{8,520},{16,528},{24,536},{32,544},{40,552},{48,560},{56,5... | collective-permute-start | bytes 122888 | tf_op jit(solution)/shard_map/ppermute | solution.py:27
  209.4 4.4 %collective-permute-done.35 = f32[5,16,128]{2,1,0:T(8,128)S(1)} collective-permute-done((f32[5,16,128]{2,1,0:T(8,128)S(1)}, f32[5,16,128]{2,1,0:T(8,128)S(1)}, u32[]{:S(2)}, u32[]{:S(2)}) %collective-permute-start.35) | collective-permute-done | bytes 40992 | tf_op jit(solution)/shard_map/ppermute | solution.py:27
  215.3 2.0 fusion.43
  217.9 1.9 collective-permute-start.36
  219.9 3.9 %collective-permute-start.37 = (f32[5,1,16,128]{3,1,0,2:T(1,128)S(1)}, f32[5,1,16,128]{3,1,0,2:T(1,128)S(1)}, u32[]{:S(2)}, u32[]{:S(2)}) collective-permute-start(f32[5,1,16,128]{3,1,0,2:T(1,128)S(1)} %get-tuple-element.8), channel_id=1, source_target_pairs={{0,8},{8,16},{16,24},{24,32},{32,40},{40,48},{48,56},{56,64},{64,7... | collective-permute-start | bytes 122888 | tf_op jit(solution)/shard_map/ppermute | solution.py:17
  223.8 1.9 collective-permute-start.38
  225.7 2.4 collective-permute-start.46
  229.9 1.9 collective-permute-start.39
  233.2 1.9 collective-permute-start.47
  235.2 4.8 %collective-permute-done.39 = f32[5,16,128]{2,1,0:T(8,128)S(1)} collective-permute-done((f32[5,16,128]{2,1,0:T(8,128)S(1)}, f32[5,16,128]{2,1,0:T(8,128)S(1)}, u32[]{:S(2)}, u32[]{:S(2)}) %collective-permute-start.39) | collective-permute-done | bytes 40992 | tf_op jit(solution)/shard_map/ppermute | solution.py:27
  243.5 2.1 collective-permute-start.48
  245.7 4.7 %collective-permute-done.40 = f32[5,16,128]{2,1,0:T(8,128)S(1)} collective-permute-done((f32[5,16,128]{2,1,0:T(8,128)S(1)}, f32[5,16,128]{2,1,0:T(8,128)S(1)}, u32[]{:S(2)}, u32[]{:S(2)}) %collective-permute-start.40) | collective-permute-done | bytes 40992 | tf_op jit(solution)/shard_map/ppermute | solution.py:27
  256.1 2.5 collective-permute-done.41
  264.1 3.3 %collective-permute-done.42 = f32[5,16,128]{2,1,0:T(8,128)S(1)} collective-permute-done((f32[5,16,128]{2,1,0:T(8,128)S(1)}, f32[5,16,128]{2,1,0:T(8,128)S(1)}, u32[]{:S(2)}, u32[]{:S(2)}) %collective-permute-start.42) | collective-permute-done | bytes 40992 | tf_op jit(solution)/shard_map/ppermute | solution.py:27
  267.4 1.9 collective-permute-start.43
  269.4 2.0 collective-permute-done.50
  271.4 3.9 %collective-permute-start.51 = (f32[5,16,128]{2,1,0:T(8,128)S(1)}, f32[5,16,128]{2,1,0:T(8,128)S(1)}, u32[]{:S(2)}, u32[]{:S(2)}) collective-permute-start(f32[5,16,128]{2,1,0:T(8,128)S(1)} %broadcast_select_fusion.3), channel_id=1, source_target_pairs={{0,128},{8,136},{16,144},{24,152},{32,160},{40,168},{48,176},{56,1... | collective-permute-start | bytes 122888 | tf_op jit(solution)/shard_map/ppermute | solution.py:27
  275.2 3.4 %collective-permute-done.43 = f32[5,16,128]{2,1,0:T(8,128)S(1)} collective-permute-done((f32[5,16,128]{2,1,0:T(8,128)S(1)}, f32[5,16,128]{2,1,0:T(8,128)S(1)}, u32[]{:S(2)}, u32[]{:S(2)}) %collective-permute-start.43) | collective-permute-done | bytes 40992 | tf_op jit(solution)/shard_map/ppermute | solution.py:27
  278.7 3.5 %collective-permute-start.44 = (f32[5,16,128]{2,1,0:T(8,128)S(1)}, f32[5,16,128]{2,1,0:T(8,128)S(1)}, u32[]{:S(2)}, u32[]{:S(2)}) collective-permute-start(f32[5,16,128]{2,1,0:T(8,128)S(1)} %broadcast_select_fusion.10), channel_id=1, source_target_pairs={{0,256},{8,264},{16,272},{24,280},{32,288},{40,296},{48,304},{56,3... | collective-permute-start | bytes 122888 | tf_op jit(solution)/shard_map/ppermute | solution.py:27
  283.1 4.9 %collective-permute-start.52 = (f32[5,16,128]{2,1,0:T(8,128)S(1)}, f32[5,16,128]{2,1,0:T(8,128)S(1)}, u32[]{:S(2)}, u32[]{:S(2)}) collective-permute-start(f32[5,16,128]{2,1,0:T(8,128)S(1)} %broadcast_select_fusion.4), channel_id=1, source_target_pairs={{0,256},{8,264},{16,272},{24,280},{32,288},{40,296},{48,304},{56,3... | collective-permute-start | bytes 122888 | tf_op jit(solution)/shard_map/ppermute | solution.py:27
  289.4 5.4 %collective-permute-start.45 = (f32[5,16,128]{2,1,0:T(8,128)S(1)}, f32[5,16,128]{2,1,0:T(8,128)S(1)}, u32[]{:S(2)}, u32[]{:S(2)}) collective-permute-start(f32[5,16,128]{2,1,0:T(8,128)S(1)} %broadcast_select_fusion.11), channel_id=1, source_target_pairs={{0,512},{8,520},{16,528},{24,536},{32,544},{40,552},{48,560},{56,5... | collective-permute-start | bytes 122888 | tf_op jit(solution)/shard_map/ppermute | solution.py:27
  294.8 5.4 %collective-permute-start.53 = (f32[5,16,128]{2,1,0:T(8,128)S(1)}, f32[5,16,128]{2,1,0:T(8,128)S(1)}, u32[]{:S(2)}, u32[]{:S(2)}) collective-permute-start(f32[5,16,128]{2,1,0:T(8,128)S(1)} %broadcast_select_fusion.5), channel_id=1, source_target_pairs={{0,512},{8,520},{16,528},{24,536},{32,544},{40,552},{48,560},{56,5... | collective-permute-start | bytes 122888 | tf_op jit(solution)/shard_map/ppermute | solution.py:27
  300.4 4.6 %collective-permute-done.53 = f32[5,16,128]{2,1,0:T(8,128)S(1)} collective-permute-done((f32[5,16,128]{2,1,0:T(8,128)S(1)}, f32[5,16,128]{2,1,0:T(8,128)S(1)}, u32[]{:S(2)}, u32[]{:S(2)}) %collective-permute-start.53) | collective-permute-done | bytes 40992 | tf_op jit(solution)/shard_map/ppermute | solution.py:27
  306.6 2.1 fusion.39
  (151 shorter events, 67.9 us)
Async XLA Ops:
  0.0 6.8 %copy-start = (f32[5,16,16,128]{3,2,1,0:T(8,128)S(1)}, f32[5,16,16,128]{3,2,1,0:T(8,128)}, u32[]{:S(2)}) copy-start(f32[5,16,16,128]{3,2,1,0:T(8,128)} %param.4) | copy-start | bytes 1966084
  1.4 45.2 %collective-permute-start.2 = (f32[5,16,1,128]{3,1,0,2:T(8,128)S(1)}, f32[5,16,1,128]{3,1,0,2:T(8,128)S(1)}, u32[]{:S(2)}, u32[]{:S(2)}) collective-permute-start(f32[5,16,1,128]{3,1,0,2:T(8,128)S(1)} %get-tuple-element.35), channel_id=1, source_target_pairs={{1,0},{2,1},{3,2},{4,3},{5,4},{6,5},{7,6},{9,8},{10,9},{11,10},{12... | collective-permute-start | bytes 122888 | tf_op jit(solution)/shard_map/ppermute | solution.py:20
  4.9 43.7 %collective-permute-start.10 = (f32[5,16,1,128]{3,1,0,2:T(8,128)S(1)}, f32[5,16,1,128]{3,1,0,2:T(8,128)S(1)}, u32[]{:S(2)}, u32[]{:S(2)}) collective-permute-start(f32[5,16,1,128]{3,1,0,2:T(8,128)S(1)} %get-tuple-element.36), channel_id=1, source_target_pairs={{0,1},{1,2},{2,3},{3,4},{4,5},{5,6},{6,7},{8,9},{9,10},{10,11},{11... | collective-permute-start | bytes 122888 | tf_op jit(solution)/shard_map/ppermute | solution.py:17
  7.5 43.0 %collective-permute-start = (f32[5,1,16,128]{3,1,0,2:T(1,128)}, f32[5,1,16,128]{3,1,0,2:T(1,128)S(1)}, u32[]{:S(2)}, u32[]{:S(2)}) collective-permute-start(f32[5,1,16,128]{3,1,0,2:T(1,128)} %copy.8), channel_id=1, source_target_pairs={{8,0},{16,8},{24,16},{32,24},{40,32},{48,40},{56,48},{64,56},{72,6... | collective-permute-start | bytes 122888 | tf_op jit(solution)/shard_map/ppermute | solution.py:20
  24.4 2.6 copy-start.9
  25.1 25.5 %collective-permute-start.1 = (f32[5,1,16,128]{3,1,0,2:T(1,128)}, f32[5,1,16,128]{3,1,0,2:T(1,128)S(1)}, u32[]{:S(2)}, u32[]{:S(2)}) collective-permute-start(f32[5,1,16,128]{3,1,0,2:T(1,128)} %copy.9), channel_id=1, source_target_pairs={{0,8},{8,16},{16,24},{24,32},{32,40},{40,48},{48,56},{56,64},{64,7... | collective-permute-start | bytes 122888 | tf_op jit(solution)/shard_map/ppermute | solution.py:17
  31.8 0.7 copy-start.8
  46.6 10.1 %collective-permute-start.3 = (f32[5,16,128]{2,1,0:T(8,128)S(1)}, f32[5,16,128]{2,1,0:T(8,128)S(1)}, u32[]{:S(2)}, u32[]{:S(2)}) collective-permute-start(f32[5,16,128]{2,1,0:T(8,128)S(1)} %bitcast.177), channel_id=1, source_target_pairs={{0,8},{8,16},{16,24},{24,32},{32,40},{40,48},{48,56},{56,64},{64,7... | collective-permute-start | bytes 122888 | tf_op jit(solution)/shard_map/ppermute | solution.py:27
  48.6 10.1 %collective-permute-start.11 = (f32[5,16,128]{2,1,0:T(8,128)S(1)}, f32[5,16,128]{2,1,0:T(8,128)S(1)}, u32[]{:S(2)}, u32[]{:S(2)}) collective-permute-start(f32[5,16,128]{2,1,0:T(8,128)S(1)} %bitcast.176), channel_id=1, source_target_pairs={{0,8},{8,16},{16,24},{24,32},{32,40},{40,48},{48,56},{56,64},{64,7... | collective-permute-start | bytes 122888 | tf_op jit(solution)/shard_map/ppermute | solution.py:27
  56.8 10.7 %collective-permute-start.4 = (f32[5,16,128]{2,1,0:T(8,128)S(1)}, f32[5,16,128]{2,1,0:T(8,128)S(1)}, u32[]{:S(2)}, u32[]{:S(2)}) collective-permute-start(f32[5,16,128]{2,1,0:T(8,128)S(1)} %broadcast_select_fusion.30), channel_id=1, source_target_pairs={{0,16},{8,24},{16,32},{24,40},{32,48},{40,56},{48,64},{56,72},{64,... | collective-permute-start | bytes 122888 | tf_op jit(solution)/shard_map/ppermute | solution.py:27
  58.7 10.6 %collective-permute-start.12 = (f32[5,16,128]{2,1,0:T(8,128)S(1)}, f32[5,16,128]{2,1,0:T(8,128)S(1)}, u32[]{:S(2)}, u32[]{:S(2)}) collective-permute-start(f32[5,16,128]{2,1,0:T(8,128)S(1)} %broadcast_select_fusion.24), channel_id=1, source_target_pairs={{0,16},{8,24},{16,32},{24,40},{32,48},{40,56},{48,64},{56,72},{64,... | collective-permute-start | bytes 122888 | tf_op jit(solution)/shard_map/ppermute | solution.py:27
  67.4 8.0 %collective-permute-start.5 = (f32[5,16,128]{2,1,0:T(8,128)S(1)}, f32[5,16,128]{2,1,0:T(8,128)S(1)}, u32[]{:S(2)}, u32[]{:S(2)}) collective-permute-start(f32[5,16,128]{2,1,0:T(8,128)S(1)} %broadcast_select_fusion.31), channel_id=1, source_target_pairs={{0,32},{8,40},{16,48},{24,56},{32,64},{40,72},{48,80},{56,88},{64,... | collective-permute-start | bytes 122888 | tf_op jit(solution)/shard_map/ppermute | solution.py:27
  69.4 8.8 %collective-permute-start.13 = (f32[5,16,128]{2,1,0:T(8,128)S(1)}, f32[5,16,128]{2,1,0:T(8,128)S(1)}, u32[]{:S(2)}, u32[]{:S(2)}) collective-permute-start(f32[5,16,128]{2,1,0:T(8,128)S(1)} %broadcast_select_fusion.25), channel_id=1, source_target_pairs={{0,32},{8,40},{16,48},{24,56},{32,64},{40,72},{48,80},{56,88},{64,... | collective-permute-start | bytes 122888 | tf_op jit(solution)/shard_map/ppermute | solution.py:27
  75.4 42.2 %copy-start.7 = (f32[3,2,16,16]{3,2,1,0:T(8,128)S(1)}, f32[3,2,16,16]{3,2,1,0:T(8,128)}, u32[]{:S(2)}) copy-start(f32[3,2,16,16]{3,2,1,0:T(8,128)} %param.6) | copy-start | bytes 18436
  75.4 9.6 %collective-permute-start.6 = (f32[5,16,128]{2,1,0:T(8,128)S(1)}, f32[5,16,128]{2,1,0:T(8,128)S(1)}, u32[]{:S(2)}, u32[]{:S(2)}) collective-permute-start(f32[5,16,128]{2,1,0:T(8,128)S(1)} %broadcast_select_fusion.32), channel_id=1, source_target_pairs={{0,64},{8,72},{16,80},{24,88},{32,96},{40,104},{48,112},{56,120},{... | collective-permute-start | bytes 122888 | tf_op jit(solution)/shard_map/ppermute | solution.py:27
  78.1 43.8 %copy-start.5 = (f32[5,16,15,128]{3,1,0,2:T(8,128)S(1)}, f32[5,16,15,128]{3,1,0,2:T(8,128)}, u32[]{:S(2)}) copy-start(f32[5,16,15,128]{3,1,0,2:T(8,128)} %get-tuple-element.34) | copy-start | bytes 1843204
  78.2 43.8 %copy-start.4 = (f32[5,16,15,128]{3,1,0,2:T(8,128)S(1)}, f32[5,16,15,128]{3,1,0,2:T(8,128)}, u32[]{:S(2)}) copy-start(f32[5,16,15,128]{3,1,0,2:T(8,128)} %get-tuple-element.33) | copy-start | bytes 1843204
  78.2 9.2 %collective-permute-start.14 = (f32[5,16,128]{2,1,0:T(8,128)S(1)}, f32[5,16,128]{2,1,0:T(8,128)S(1)}, u32[]{:S(2)}, u32[]{:S(2)}) collective-permute-start(f32[5,16,128]{2,1,0:T(8,128)S(1)} %broadcast_select_fusion.26), channel_id=1, source_target_pairs={{0,64},{8,72},{16,80},{24,88},{32,96},{40,104},{48,112},{56,120},{... | collective-permute-start | bytes 122888 | tf_op jit(solution)/shard_map/ppermute | solution.py:27
  85.1 11.1 %collective-permute-start.7 = (f32[5,16,128]{2,1,0:T(8,128)S(1)}, f32[5,16,128]{2,1,0:T(8,128)S(1)}, u32[]{:S(2)}, u32[]{:S(2)}) collective-permute-start(f32[5,16,128]{2,1,0:T(8,128)S(1)} %broadcast_select_fusion.33), channel_id=1, source_target_pairs={{0,128},{8,136},{16,144},{24,152},{32,160},{40,168},{48,176},{56,1... | collective-permute-start | bytes 122888 | tf_op jit(solution)/shard_map/ppermute | solution.py:27
  87.3 11.7 %collective-permute-start.15 = (f32[5,16,128]{2,1,0:T(8,128)S(1)}, f32[5,16,128]{2,1,0:T(8,128)S(1)}, u32[]{:S(2)}, u32[]{:S(2)}) collective-permute-start(f32[5,16,128]{2,1,0:T(8,128)S(1)} %broadcast_select_fusion.27), channel_id=1, source_target_pairs={{0,128},{8,136},{16,144},{24,152},{32,160},{40,168},{48,176},{56,1... | collective-permute-start | bytes 122888 | tf_op jit(solution)/shard_map/ppermute | solution.py:27
  96.2 11.2 %collective-permute-start.8 = (f32[5,16,128]{2,1,0:T(8,128)S(1)}, f32[5,16,128]{2,1,0:T(8,128)S(1)}, u32[]{:S(2)}, u32[]{:S(2)}) collective-permute-start(f32[5,16,128]{2,1,0:T(8,128)S(1)} %broadcast_select_fusion.34), channel_id=1, source_target_pairs={{0,256},{8,264},{16,272},{24,280},{32,288},{40,296},{48,304},{56,3... | collective-permute-start | bytes 122888 | tf_op jit(solution)/shard_map/ppermute | solution.py:27
  99.1 12.3 %collective-permute-start.16 = (f32[5,16,128]{2,1,0:T(8,128)S(1)}, f32[5,16,128]{2,1,0:T(8,128)S(1)}, u32[]{:S(2)}, u32[]{:S(2)}) collective-permute-start(f32[5,16,128]{2,1,0:T(8,128)S(1)} %broadcast_select_fusion.28), channel_id=1, source_target_pairs={{0,256},{8,264},{16,272},{24,280},{32,288},{40,296},{48,304},{56,3... | collective-permute-start | bytes 122888 | tf_op jit(solution)/shard_map/ppermute | solution.py:27
  107.5 10.2 %collective-permute-start.9 = (f32[5,16,128]{2,1,0:T(8,128)S(1)}, f32[5,16,128]{2,1,0:T(8,128)S(1)}, u32[]{:S(2)}, u32[]{:S(2)}) collective-permute-start(f32[5,16,128]{2,1,0:T(8,128)S(1)} %broadcast_select_fusion.35), channel_id=1, source_target_pairs={{0,512},{8,520},{16,528},{24,536},{32,544},{40,552},{48,560},{56,5... | collective-permute-start | bytes 122888 | tf_op jit(solution)/shard_map/ppermute | solution.py:27
  111.4 10.4 %collective-permute-start.17 = (f32[5,16,128]{2,1,0:T(8,128)S(1)}, f32[5,16,128]{2,1,0:T(8,128)S(1)}, u32[]{:S(2)}, u32[]{:S(2)}) collective-permute-start(f32[5,16,128]{2,1,0:T(8,128)S(1)} %broadcast_select_fusion.29), channel_id=1, source_target_pairs={{0,512},{8,520},{16,528},{24,536},{32,544},{40,552},{48,560},{56,5... | collective-permute-start | bytes 122888 | tf_op jit(solution)/shard_map/ppermute | solution.py:27
  122.0 1.4 copy-start.6
  122.1 1.3 copy-start.1
  122.1 1.5 copy-start.2
  122.1 1.7 copy-start.3
  126.4 14.0 %collective-permute-start.18 = (f32[5,1,16,128]{3,1,0,2:T(1,128)S(1)}, f32[5,1,16,128]{3,1,0,2:T(1,128)S(1)}, u32[]{:S(2)}, u32[]{:S(2)}) collective-permute-start(f32[5,1,16,128]{3,1,0,2:T(1,128)S(1)} %get-tuple-element.19), channel_id=1, source_target_pairs={{8,0},{16,8},{24,16},{32,24},{40,32},{48,40},{56,48},{64,56},{72,6... | collective-permute-start | bytes 122888 | tf_op jit(solution)/shard_map/ppermute | solution.py:20
  128.4 12.1 %collective-permute-start.19 = (f32[5,1,16,128]{3,1,0,2:T(1,128)S(1)}, f32[5,1,16,128]{3,1,0,2:T(1,128)S(1)}, u32[]{:S(2)}, u32[]{:S(2)}) collective-permute-start(f32[5,1,16,128]{3,1,0,2:T(1,128)S(1)} %get-tuple-element.20), channel_id=1, source_target_pairs={{0,8},{8,16},{16,24},{24,32},{32,40},{40,48},{48,56},{56,64},{64,7... | collective-permute-start | bytes 122888 | tf_op jit(solution)/shard_map/ppermute | solution.py:17
  132.3 6.2 %collective-permute-start.20 = (f32[5,16,1,128]{3,1,0,2:T(8,128)S(1)}, f32[5,16,1,128]{3,1,0,2:T(8,128)S(1)}, u32[]{:S(2)}, u32[]{:S(2)}) collective-permute-start(f32[5,16,1,128]{3,1,0,2:T(8,128)S(1)} %get-tuple-element.23), channel_id=1, source_target_pairs={{1,0},{2,1},{3,2},{4,3},{5,4},{6,5},{7,6},{9,8},{10,9},{11,10},{12... | collective-permute-start | bytes 122888 | tf_op jit(solution)/shard_map/ppermute | solution.py:20
  134.2 7.7 %collective-permute-start.28 = (f32[5,16,1,128]{3,1,0,2:T(8,128)S(1)}, f32[5,16,1,128]{3,1,0,2:T(8,128)S(1)}, u32[]{:S(2)}, u32[]{:S(2)}) collective-permute-start(f32[5,16,1,128]{3,1,0,2:T(8,128)S(1)} %get-tuple-element.24), channel_id=1, source_target_pairs={{0,1},{1,2},{2,3},{3,4},{4,5},{5,6},{6,7},{8,9},{9,10},{10,11},{11... | collective-permute-start | bytes 122888 | tf_op jit(solution)/shard_map/ppermute | solution.py:17
  138.5 10.1 %collective-permute-start.21 = (f32[5,16,128]{2,1,0:T(8,128)S(1)}, f32[5,16,128]{2,1,0:T(8,128)S(1)}, u32[]{:S(2)}, u32[]{:S(2)}) collective-permute-start(f32[5,16,128]{2,1,0:T(8,128)S(1)} %bitcast.181), channel_id=1, source_target_pairs={{0,8},{8,16},{16,24},{24,32},{32,40},{40,48},{48,56},{56,64},{64,7... | collective-permute-start | bytes 122888 | tf_op jit(solution)/shard_map/ppermute | solution.py:27
  141.9 10.3 %collective-permute-start.29 = (f32[5,16,128]{2,1,0:T(8,128)S(1)}, f32[5,16,128]{2,1,0:T(8,128)S(1)}, u32[]{:S(2)}, u32[]{:S(2)}) collective-permute-start(f32[5,16,128]{2,1,0:T(8,128)S(1)} %bitcast.180), channel_id=1, source_target_pairs={{0,8},{8,16},{16,24},{24,32},{32,40},{40,48},{48,56},{56,64},{64,7... | collective-permute-start | bytes 122888 | tf_op jit(solution)/shard_map/ppermute | solution.py:27
  148.7 10.4 %collective-permute-start.22 = (f32[5,16,128]{2,1,0:T(8,128)S(1)}, f32[5,16,128]{2,1,0:T(8,128)S(1)}, u32[]{:S(2)}, u32[]{:S(2)}) collective-permute-start(f32[5,16,128]{2,1,0:T(8,128)S(1)} %broadcast_select_fusion.18), channel_id=1, source_target_pairs={{0,16},{8,24},{16,32},{24,40},{32,48},{40,56},{48,64},{56,72},{64,... | collective-permute-start | bytes 122888 | tf_op jit(solution)/shard_map/ppermute | solution.py:27
  152.2 10.4 %collective-permute-start.30 = (f32[5,16,128]{2,1,0:T(8,128)S(1)}, f32[5,16,128]{2,1,0:T(8,128)S(1)}, u32[]{:S(2)}, u32[]{:S(2)}) collective-permute-start(f32[5,16,128]{2,1,0:T(8,128)S(1)} %broadcast_select_fusion.12), channel_id=1, source_target_pairs={{0,16},{8,24},{16,32},{24,40},{32,48},{40,56},{48,64},{56,72},{64,... | collective-permute-start | bytes 122888 | tf_op jit(solution)/shard_map/ppermute | solution.py:27
  159.1 8.0 %collective-permute-start.23 = (f32[5,16,128]{2,1,0:T(8,128)S(1)}, f32[5,16,128]{2,1,0:T(8,128)S(1)}, u32[]{:S(2)}, u32[]{:S(2)}) collective-permute-start(f32[5,16,128]{2,1,0:T(8,128)S(1)} %broadcast_select_fusion.19), channel_id=1, source_target_pairs={{0,32},{8,40},{16,48},{24,56},{32,64},{40,72},{48,80},{56,88},{64,... | collective-permute-start | bytes 122888 | tf_op jit(solution)/shard_map/ppermute | solution.py:27
  162.6 8.1 %collective-permute-start.31 = (f32[5,16,128]{2,1,0:T(8,128)S(1)}, f32[5,16,128]{2,1,0:T(8,128)S(1)}, u32[]{:S(2)}, u32[]{:S(2)}) collective-permute-start(f32[5,16,128]{2,1,0:T(8,128)S(1)} %broadcast_select_fusion.13), channel_id=1, source_target_pairs={{0,32},{8,40},{16,48},{24,56},{32,64},{40,72},{48,80},{56,88},{64,... | collective-permute-start | bytes 122888 | tf_op jit(solution)/shard_map/ppermute | solution.py:27
  167.1 9.0 %collective-permute-start.24 = (f32[5,16,128]{2,1,0:T(8,128)S(1)}, f32[5,16,128]{2,1,0:T(8,128)S(1)}, u32[]{:S(2)}, u32[]{:S(2)}) collective-permute-start(f32[5,16,128]{2,1,0:T(8,128)S(1)} %broadcast_select_fusion.20), channel_id=1, source_target_pairs={{0,64},{8,72},{16,80},{24,88},{32,96},{40,104},{48,112},{56,120},{... | collective-permute-start | bytes 122888 | tf_op jit(solution)/shard_map/ppermute | solution.py:27
  170.7 8.9 %collective-permute-start.32 = (f32[5,16,128]{2,1,0:T(8,128)S(1)}, f32[5,16,128]{2,1,0:T(8,128)S(1)}, u32[]{:S(2)}, u32[]{:S(2)}) collective-permute-start(f32[5,16,128]{2,1,0:T(8,128)S(1)} %broadcast_select_fusion.14), channel_id=1, source_target_pairs={{0,64},{8,72},{16,80},{24,88},{32,96},{40,104},{48,112},{56,120},{... | collective-permute-start | bytes 122888 | tf_op jit(solution)/shard_map/ppermute | solution.py:27
  176.1 11.2 %collective-permute-start.25 = (f32[5,16,128]{2,1,0:T(8,128)S(1)}, f32[5,16,128]{2,1,0:T(8,128)S(1)}, u32[]{:S(2)}, u32[]{:S(2)}) collective-permute-start(f32[5,16,128]{2,1,0:T(8,128)S(1)} %broadcast_select_fusion.21), channel_id=1, source_target_pairs={{0,128},{8,136},{16,144},{24,152},{32,160},{40,168},{48,176},{56,1... | collective-permute-start | bytes 122888 | tf_op jit(solution)/shard_map/ppermute | solution.py:27
  179.6 11.9 %collective-permute-start.33 = (f32[5,16,128]{2,1,0:T(8,128)S(1)}, f32[5,16,128]{2,1,0:T(8,128)S(1)}, u32[]{:S(2)}, u32[]{:S(2)}) collective-permute-start(f32[5,16,128]{2,1,0:T(8,128)S(1)} %broadcast_select_fusion.15), channel_id=1, source_target_pairs={{0,128},{8,136},{16,144},{24,152},{32,160},{40,168},{48,176},{56,1... | collective-permute-start | bytes 122888 | tf_op jit(solution)/shard_map/ppermute | solution.py:27
  187.3 10.9 %collective-permute-start.26 = (f32[5,16,128]{2,1,0:T(8,128)S(1)}, f32[5,16,128]{2,1,0:T(8,128)S(1)}, u32[]{:S(2)}, u32[]{:S(2)}) collective-permute-start(f32[5,16,128]{2,1,0:T(8,128)S(1)} %broadcast_select_fusion.22), channel_id=1, source_target_pairs={{0,256},{8,264},{16,272},{24,280},{32,288},{40,296},{48,304},{56,3... | collective-permute-start | bytes 122888 | tf_op jit(solution)/shard_map/ppermute | solution.py:27
  191.5 12.0 %collective-permute-start.34 = (f32[5,16,128]{2,1,0:T(8,128)S(1)}, f32[5,16,128]{2,1,0:T(8,128)S(1)}, u32[]{:S(2)}, u32[]{:S(2)}) collective-permute-start(f32[5,16,128]{2,1,0:T(8,128)S(1)} %broadcast_select_fusion.16), channel_id=1, source_target_pairs={{0,256},{8,264},{16,272},{24,280},{32,288},{40,296},{48,304},{56,3... | collective-permute-start | bytes 122888 | tf_op jit(solution)/shard_map/ppermute | solution.py:27
  198.2 11.0 %collective-permute-start.27 = (f32[5,16,128]{2,1,0:T(8,128)S(1)}, f32[5,16,128]{2,1,0:T(8,128)S(1)}, u32[]{:S(2)}, u32[]{:S(2)}) collective-permute-start(f32[5,16,128]{2,1,0:T(8,128)S(1)} %broadcast_select_fusion.23), channel_id=1, source_target_pairs={{0,512},{8,520},{16,528},{24,536},{32,544},{40,552},{48,560},{56,5... | collective-permute-start | bytes 122888 | tf_op jit(solution)/shard_map/ppermute | solution.py:27
  203.6 10.2 %collective-permute-start.35 = (f32[5,16,128]{2,1,0:T(8,128)S(1)}, f32[5,16,128]{2,1,0:T(8,128)S(1)}, u32[]{:S(2)}, u32[]{:S(2)}) collective-permute-start(f32[5,16,128]{2,1,0:T(8,128)S(1)} %broadcast_select_fusion.17), channel_id=1, source_target_pairs={{0,512},{8,520},{16,528},{24,536},{32,544},{40,552},{48,560},{56,5... | collective-permute-start | bytes 122888 | tf_op jit(solution)/shard_map/ppermute | solution.py:27
  217.9 13.9 %collective-permute-start.36 = (f32[5,1,16,128]{3,1,0,2:T(1,128)S(1)}, f32[5,1,16,128]{3,1,0,2:T(1,128)S(1)}, u32[]{:S(2)}, u32[]{:S(2)}) collective-permute-start(f32[5,1,16,128]{3,1,0,2:T(1,128)S(1)} %get-tuple-element.7), channel_id=1, source_target_pairs={{8,0},{16,8},{24,16},{32,24},{40,32},{48,40},{56,48},{64,56},{72,6... | collective-permute-start | bytes 122888 | tf_op jit(solution)/shard_map/ppermute | solution.py:20
  219.9 11.9 %collective-permute-start.37 = (f32[5,1,16,128]{3,1,0,2:T(1,128)S(1)}, f32[5,1,16,128]{3,1,0,2:T(1,128)S(1)}, u32[]{:S(2)}, u32[]{:S(2)}) collective-permute-start(f32[5,1,16,128]{3,1,0,2:T(1,128)S(1)} %get-tuple-element.8), channel_id=1, source_target_pairs={{0,8},{8,16},{16,24},{24,32},{32,40},{40,48},{48,56},{56,64},{64,7... | collective-permute-start | bytes 122888 | tf_op jit(solution)/shard_map/ppermute | solution.py:17
  223.8 6.1 %collective-permute-start.38 = (f32[5,16,1,128]{3,1,0,2:T(8,128)S(1)}, f32[5,16,1,128]{3,1,0,2:T(8,128)S(1)}, u32[]{:S(2)}, u32[]{:S(2)}) collective-permute-start(f32[5,16,1,128]{3,1,0,2:T(8,128)S(1)} %get-tuple-element.11), channel_id=1, source_target_pairs={{1,0},{2,1},{3,2},{4,3},{5,4},{6,5},{7,6},{9,8},{10,9},{11,10},{12... | collective-permute-start | bytes 122888 | tf_op jit(solution)/shard_map/ppermute | solution.py:20
  225.7 7.5 %collective-permute-start.46 = (f32[5,16,1,128]{3,1,0,2:T(8,128)S(1)}, f32[5,16,1,128]{3,1,0,2:T(8,128)S(1)}, u32[]{:S(2)}, u32[]{:S(2)}) collective-permute-start(f32[5,16,1,128]{3,1,0,2:T(8,128)S(1)} %get-tuple-element.12), channel_id=1, source_target_pairs={{0,1},{1,2},{2,3},{3,4},{4,5},{5,6},{6,7},{8,9},{9,10},{10,11},{11... | collective-permute-start | bytes 122888 | tf_op jit(solution)/shard_map/ppermute | solution.py:17
  229.9 10.1 %collective-permute-start.39 = (f32[5,16,128]{2,1,0:T(8,128)S(1)}, f32[5,16,128]{2,1,0:T(8,128)S(1)}, u32[]{:S(2)}, u32[]{:S(2)}) collective-permute-start(f32[5,16,128]{2,1,0:T(8,128)S(1)} %bitcast.179), channel_id=1, source_target_pairs={{0,8},{8,16},{16,24},{24,32},{32,40},{40,48},{48,56},{56,64},{64,7... | collective-permute-start | bytes 122888 | tf_op jit(solution)/shard_map/ppermute | solution.py:27
  233.2 10.3 %collective-permute-start.47 = (f32[5,16,128]{2,1,0:T(8,128)S(1)}, f32[5,16,128]{2,1,0:T(8,128)S(1)}, u32[]{:S(2)}, u32[]{:S(2)}) collective-permute-start(f32[5,16,128]{2,1,0:T(8,128)S(1)} %bitcast.178), channel_id=1, source_target_pairs={{0,8},{8,16},{16,24},{24,32},{32,40},{40,48},{48,56},{56,64},{64,7... | collective-permute-start | bytes 122888 | tf_op jit(solution)/shard_map/ppermute | solution.py:27
  240.0 10.4 %collective-permute-start.40 = (f32[5,16,128]{2,1,0:T(8,128)S(1)}, f32[5,16,128]{2,1,0:T(8,128)S(1)}, u32[]{:S(2)}, u32[]{:S(2)}) collective-permute-start(f32[5,16,128]{2,1,0:T(8,128)S(1)} %broadcast_select_fusion.6), channel_id=1, source_target_pairs={{0,16},{8,24},{16,32},{24,40},{32,48},{40,56},{48,64},{56,72},{64,... | collective-permute-start | bytes 122888 | tf_op jit(solution)/shard_map/ppermute | solution.py:27
  243.5 10.6 %collective-permute-start.48 = (f32[5,16,128]{2,1,0:T(8,128)S(1)}, f32[5,16,128]{2,1,0:T(8,128)S(1)}, u32[]{:S(2)}, u32[]{:S(2)}) collective-permute-start(f32[5,16,128]{2,1,0:T(8,128)S(1)} %broadcast_select_fusion), channel_id=1, source_target_pairs={{0,16},{8,24},{16,32},{24,40},{32,48},{40,56},{48,64},{56,72},{64,... | collective-permute-start | bytes 122888 | tf_op jit(solution)/shard_map/ppermute | solution.py:27
  250.4 8.1 %collective-permute-start.41 = (f32[5,16,128]{2,1,0:T(8,128)S(1)}, f32[5,16,128]{2,1,0:T(8,128)S(1)}, u32[]{:S(2)}, u32[]{:S(2)}) collective-permute-start(f32[5,16,128]{2,1,0:T(8,128)S(1)} %broadcast_select_fusion.7), channel_id=1, source_target_pairs={{0,32},{8,40},{16,48},{24,56},{32,64},{40,72},{48,80},{56,88},{64,... | collective-permute-start | bytes 122888 | tf_op jit(solution)/shard_map/ppermute | solution.py:27
  254.2 8.0 %collective-permute-start.49 = (f32[5,16,128]{2,1,0:T(8,128)S(1)}, f32[5,16,128]{2,1,0:T(8,128)S(1)}, u32[]{:S(2)}, u32[]{:S(2)}) collective-permute-start(f32[5,16,128]{2,1,0:T(8,128)S(1)} %broadcast_select_fusion.1), channel_id=1, source_target_pairs={{0,32},{8,40},{16,48},{24,56},{32,64},{40,72},{48,80},{56,88},{64,... | collective-permute-start | bytes 122888 | tf_op jit(solution)/shard_map/ppermute | solution.py:27
  258.5 8.9 %collective-permute-start.42 = (f32[5,16,128]{2,1,0:T(8,128)S(1)}, f32[5,16,128]{2,1,0:T(8,128)S(1)}, u32[]{:S(2)}, u32[]{:S(2)}) collective-permute-start(f32[5,16,128]{2,1,0:T(8,128)S(1)} %broadcast_select_fusion.8), channel_id=1, source_target_pairs={{0,64},{8,72},{16,80},{24,88},{32,96},{40,104},{48,112},{56,120},{... | collective-permute-start | bytes 122888 | tf_op jit(solution)/shard_map/ppermute | solution.py:27
  262.2 9.2 %collective-permute-start.50 = (f32[5,16,128]{2,1,0:T(8,128)S(1)}, f32[5,16,128]{2,1,0:T(8,128)S(1)}, u32[]{:S(2)}, u32[]{:S(2)}) collective-permute-start(f32[5,16,128]{2,1,0:T(8,128)S(1)} %broadcast_select_fusion.2), channel_id=1, source_target_pairs={{0,64},{8,72},{16,80},{24,88},{32,96},{40,104},{48,112},{56,120},{... | collective-permute-start | bytes 122888 | tf_op jit(solution)/shard_map/ppermute | solution.py:27
  267.4 11.2 %collective-permute-start.43 = (f32[5,16,128]{2,1,0:T(8,128)S(1)}, f32[5,16,128]{2,1,0:T(8,128)S(1)}, u32[]{:S(2)}, u32[]{:S(2)}) collective-permute-start(f32[5,16,128]{2,1,0:T(8,128)S(1)} %broadcast_select_fusion.9), channel_id=1, source_target_pairs={{0,128},{8,136},{16,144},{24,152},{32,160},{40,168},{48,176},{56,1... | collective-permute-start | bytes 122888 | tf_op jit(solution)/shard_map/ppermute | solution.py:27
  271.4 11.7 %collective-permute-start.51 = (f32[5,16,128]{2,1,0:T(8,128)S(1)}, f32[5,16,128]{2,1,0:T(8,128)S(1)}, u32[]{:S(2)}, u32[]{:S(2)}) collective-permute-start(f32[5,16,128]{2,1,0:T(8,128)S(1)} %broadcast_select_fusion.3), channel_id=1, source_target_pairs={{0,128},{8,136},{16,144},{24,152},{32,160},{40,168},{48,176},{56,1... | collective-permute-start | bytes 122888 | tf_op jit(solution)/shard_map/ppermute | solution.py:27
  278.7 10.7 %collective-permute-start.44 = (f32[5,16,128]{2,1,0:T(8,128)S(1)}, f32[5,16,128]{2,1,0:T(8,128)S(1)}, u32[]{:S(2)}, u32[]{:S(2)}) collective-permute-start(f32[5,16,128]{2,1,0:T(8,128)S(1)} %broadcast_select_fusion.10), channel_id=1, source_target_pairs={{0,256},{8,264},{16,272},{24,280},{32,288},{40,296},{48,304},{56,3... | collective-permute-start | bytes 122888 | tf_op jit(solution)/shard_map/ppermute | solution.py:27
  283.1 11.7 %collective-permute-start.52 = (f32[5,16,128]{2,1,0:T(8,128)S(1)}, f32[5,16,128]{2,1,0:T(8,128)S(1)}, u32[]{:S(2)}, u32[]{:S(2)}) collective-permute-start(f32[5,16,128]{2,1,0:T(8,128)S(1)} %broadcast_select_fusion.4), channel_id=1, source_target_pairs={{0,256},{8,264},{16,272},{24,280},{32,288},{40,296},{48,304},{56,3... | collective-permute-start | bytes 122888 | tf_op jit(solution)/shard_map/ppermute | solution.py:27
  289.4 10.8 %collective-permute-start.45 = (f32[5,16,128]{2,1,0:T(8,128)S(1)}, f32[5,16,128]{2,1,0:T(8,128)S(1)}, u32[]{:S(2)}, u32[]{:S(2)}) collective-permute-start(f32[5,16,128]{2,1,0:T(8,128)S(1)} %broadcast_select_fusion.11), channel_id=1, source_target_pairs={{0,512},{8,520},{16,528},{24,536},{32,544},{40,552},{48,560},{56,5... | collective-permute-start | bytes 122888 | tf_op jit(solution)/shard_map/ppermute | solution.py:27
  294.8 10.2 %collective-permute-start.53 = (f32[5,16,128]{2,1,0:T(8,128)S(1)}, f32[5,16,128]{2,1,0:T(8,128)S(1)}, u32[]{:S(2)}, u32[]{:S(2)}) collective-permute-start(f32[5,16,128]{2,1,0:T(8,128)S(1)} %broadcast_select_fusion.5), channel_id=1, source_target_pairs={{0,512},{8,520},{16,528},{24,536},{32,544},{40,552},{48,560},{56,5... | collective-permute-start | bytes 122888 | tf_op jit(solution)/shard_map/ppermute | solution.py:27
where the time goes:
time: 312 us; the launch traced here: 310 us
  starting transfers between devices  172 us (55%)
  waiting for transfers between devices  92.4 us (30%)
  matrix products  12.9 us (4%)
  between operations  11.8 us (4%)
  local copies, waits for them, and re-layouts  10.4 us (3%)
  other arithmetic  9.95 us (3%)
    ppermute x42, starting transfers between devices, shifted(): lax.ppermute(shard, axis, [(i, (i + by) % size) for i in range(size)])  128 us
    ppermute x42, waiting for transfers between devices, shifted(): lax.ppermute(shard, axis, [(i, (i + by) % size) for i in range(size)])  92.4 us
    ppermute x6, starting transfers between devices, extended(): lax.ppermute(lax.slice_in_dim(block, 0, width, axis=dim), axis, backward)  28 us
    ppermute x6, starting transfers between devices, extended(): lax.ppermute(lax.slice_in_dim(block, block.shape[dim] - width, None, axis...  16.7 us
    dot_general x9, matrix products, apply_matrix(): jnp.einsum('vw,wtar->vtar', matrix, values, precision=lax.Precision.HIGHEST)  11.9 us
  transfers between devices with their start and end apart: 54, of which 33 were waited for; matrix products, arithmetic and copies ran while one was open for 6% of the time, Pallas kernels for 0%

commit v1 on v0

v1 whole, which is shorter than its diff:
```python
import functools

import jax
import jax.numpy as jnp
from jax import lax
from jax.experimental import pallas as pl
from jax.experimental.pallas import tpu as pltpu
from jax.sharding import PartitionSpec as P

NVAR = 5
time_step = 0.25
viscosity = 0.3
SECTION_WEIGHTS = (
    (0.0, 1.0, time_step),
    (0.75, 0.25, 0.25 * time_step),
    (1.0 / 3.0, 2.0 / 3.0, 2.0 / 3.0 * time_step),
)
AXES = ("theta", "axial")
VMEM = pl.BlockSpec(memory_space=pltpu.VMEM)
SMEM = pl.BlockSpec(memory_space=pltpu.SMEM)


def write_rims(value_of, is_odd, theta_low, theta_high, core_rim, hop_rim, cells):
    for v in range(NVAR):
        theta_low[v] = value_of(v, 0)
        theta_high[v] = value_of(v, cells - 1)

    def step(t, carry):
        for v in range(NVAR):
            write_axial_rims(value_of(v, t), v, t, is_odd, core_rim, hop_rim)
        return carry

    lax.fori_loop(0, cells, step, 0)


def write_axial_rims(value, v, t, is_odd, core_rim, hop_rim):
    first, last = value[:1], value[-1:]
    core_rim[v, pl.ds(t, 1), :] = jnp.where(is_odd, first, last)
    hop_rim[v, pl.ds(t, 1), :] = jnp.where(is_odd, last, first)


def rims_kernel(place, current, theta_low, theta_high, core_rim, hop_rim):
    is_odd = place[0] % 2 == 1
    cells = current.shape[1]
    write_rims(
        lambda v, t: current[v, t], is_odd, theta_low, theta_high, core_rim, hop_rim, cells
    )


def section_kernel(section, blocks, last, *refs):
    place, flux, weights, current, conserved, before, after, core_in, hop_in, hop_own = refs[:10]
    rims = refs[11:-2]
    out, low_ghost, high_ghost = refs[10], refs[-2], refs[-1]
    index = place[0]
    is_odd = index % 2 == 1
    cells, width, radial = current.shape[1:]
    at_plane = (index == blocks // 2) | (index == blocks // 2 - 1)
    at_end = (index == 0) | (index == blocks - 1)
    inside = jnp.logical_not(at_plane | at_end)

    def put(core_side, hop_side):
        @pl.when(at_plane)
        def _():
            mix = weights[section, jnp.where(index == blocks // 2, 0, 1)]
            for v in range(NVAR):
                hop_side[v] = jnp.dot(
                    mix,
                    hop_in[v],
                    precision=lax.Precision.HIGHEST,
                    preferred_element_type=jnp.float32,
                )

        @pl.when(at_end)
        def _():
            hop_side[...] = hop_own[...]

        @pl.when(inside)
        def _():
            hop_side[...] = hop_in[...]

        core_side[...] = core_in[...]

    @pl.when(is_odd)
    def _():
        put(low_ghost, high_ghost)

    @pl.when(jnp.logical_not(is_odd))
    def _():
        put(high_ghost, low_ghost)

    keep, carry_on, push = SECTION_WEIGHTS[section]
    row = lax.broadcasted_iota(jnp.int32, (width, radial), 0)
    lane = lax.broadcasted_iota(jnp.int32, (width, radial), 1)

    def cell_row(t, minus_of, plus_of):
        slope = [None] * NVAR
        smooth = [None] * NVAR
        for w in range(NVAR):
            c = current[w, t]
            tm, tp = minus_of(w), plus_of(w)
            low = low_ghost[w, pl.ds(t, 1), :]
            high = high_ghost[w, pl.ds(t, 1), :]
            am = jnp.where(row == 0, low, pltpu.roll(c, 1, 0))
            ap = jnp.where(row == width - 1, high, pltpu.roll(c, width - 1, 0))
            rm = jnp.where(lane == 0, c, pltpu.roll(c, 1, 1))
            rp = jnp.where(lane == radial - 1, c, pltpu.roll(c, radial - 1, 1))
            total = (tm + tp) + (am + ap) + (rm + rp)
            smooth[w] = (viscosity * push) * total + (carry_on - 6.0 * viscosity * push) * c
            if section:
                smooth[w] = smooth[w] + keep * conserved[w, t]
            dt, da, dr = tp - tm, ap - am, rp - rm
            for v in range(NVAR):
                term = flux[0, v, w] * dt + flux[1, v, w] * da + flux[2, v, w] * dr
                slope[v] = term if slope[v] is None else slope[v] + term
        for v in range(NVAR):
            new = smooth[v] - (0.5 * push) * slope[v]
            out[v, t] = new
            if not last:
                write_axial_rims(new, v, t, is_odd, rims[2], rims[3])

    def step(t, carry):
        cell_row(t, lambda w: current[w, t - 1], lambda w: current[w, t + 1])
        return carry

    cell_row(0, lambda w: before[w], lambda w: current[w, 1])
    lax.fori_loop(1, cells - 1, step, 0)
    cell_row(cells - 1, lambda w: current[w, cells - 2], lambda w: after[w])
    if not last:
        for v in range(NVAR):
            rims[0][v] = out[v, 0]
            rims[1][v] = out[v, cells - 1]


def rim_shapes(current):
    nvar, cells, width, radial = current.shape
    theta_rim = jax.ShapeDtypeStruct((nvar, width, radial), jnp.float32)
    axial_rim = jax.ShapeDtypeStruct((nvar, cells, radial), jnp.float32)
    return (theta_rim, theta_rim, axial_rim, axial_rim)


def first_rims(place, current):
    return pl.pallas_call(
        rims_kernel,
        out_shape=rim_shapes(current),
        in_specs=[SMEM, VMEM],
        out_specs=(VMEM,) * 4,
        compiler_params=pltpu.CompilerParams(vmem_limit_bytes=8 << 20),
        name="rims",
    )(place, current)


def advance(section, blocks, last, place, flux, weights, current, conserved, ghosts):
    outs = (jax.ShapeDtypeStruct(current.shape, jnp.float32),)
    if not last:
        outs = outs + rim_shapes(current)
    nvar, cells, _, radial = current.shape
    return pl.pallas_call(
        functools.partial(section_kernel, section, blocks, last),
        out_shape=outs,
        in_specs=[SMEM, SMEM] + [VMEM] * 8,
        out_specs=(VMEM,) * len(outs),
        scratch_shapes=[pltpu.VMEM((nvar, cells, radial), jnp.float32)] * 2,
        compiler_params=pltpu.CompilerParams(vmem_limit_bytes=16 << 20),
        name="section",
    )(place, flux, weights, current, conserved, *ghosts)


def ring(by, sectors):
    return [(i, (i + by) % sectors) for i in range(sectors)]


def core_pairs(blocks):
    return [(a, a ^ 1) for a in range(blocks)]


FINE = 4


def spin_pairs(by, sectors, blocks):
    rotor, stator = blocks // 2 - 1, blocks // 2
    pairs = []
    for t in range(sectors):
        ahead = (t + by) % sectors
        pairs.append((t * blocks + rotor, ahead * blocks + rotor))
        pairs.append((ahead * blocks + stator, t * blocks + stator))
    return pairs


def hop_pairs(by, sectors, blocks):
    pairs = []
    for a in range(1, blocks - 1, 2):
        shift = by if a == blocks // 2 - 1 else 0
        for t in range(sectors):
            low, high = t * blocks + a, (t + shift) % sectors * blocks + a + 1
            pairs += [(low, high), (high, low)]
    return pairs


def exchange_hop(face, offset, at_plane, sectors, blocks):
    shifts = list(range(-1, FINE - 1))
    fine = (offset + 1) % FINE
    coarse = (offset + 1) // FINE % (sectors // FINE)

    def spin(by, value):
        if by == 0:
            return value
        moved = lax.ppermute(value, AXES, spin_pairs(by, sectors, blocks))
        return jnp.where(at_plane, moved, value)

    def hop(by, value):
        return lax.ppermute(value, AXES, hop_pairs(by, sectors, blocks))

    face = lax.switch(fine, [functools.partial(spin, by) for by in shifts], face)
    return lax.switch(
        coarse, [functools.partial(hop, FINE * k) for k in range(sectors // FINE)], face
    )


def local(conserved, flux_matrices, slide_weights, rotor_offsets):
    sectors, blocks = lax.axis_size("theta"), lax.axis_size("axial")
    index = lax.axis_index("axial")
    place = jnp.full((1,), index, jnp.int32)
    at_plane = (index == blocks // 2) | (index == blocks // 2 - 1)
    current, rims = conserved, first_rims(place, conserved)
    sections = len(SECTION_WEIGHTS)
    for section in range(sections):
        theta_low, theta_high, core_rim, hop_rim = rims
        before = lax.ppermute(theta_high, "theta", ring(1, sectors))
        after = lax.ppermute(theta_low, "theta", ring(-1, sectors))
        core_in = lax.ppermute(core_rim, "axial", core_pairs(blocks))
        hop_in = exchange_hop(hop_rim, rotor_offsets[section], at_plane, sectors, blocks)
        current, *rims = advance(
            section,
            blocks,
            section == sections - 1,
            place,
            flux_matrices,
            slide_weights,
            current,
            conserved,
            (before, after, core_in, hop_in, hop_rim),
        )
    return current


def solution(mesh):
    in_specs = (P(None, "theta", "axial", None), P(), P(), P())
    out_specs = P(None, "theta", "axial", None)
    return jax.shard_map(local, mesh=mesh, in_specs=in_specs, out_specs=out_specs, check_vma=False)
```

time: 312 us -> 123 us (0.39)
  the two profiles are of different devices: /device:TPU:48 before, /device:TPU:40 now
where the time goes in v1:
time: 123 us
  starting transfers between devices  62.9 us (51%)
  waiting for transfers between devices  45.3 us (37%)
  Pallas kernels  9.44 us (8%)
  local copies, waits for them, and re-layouts  2.44 us (2%)
  between operations  2.23 us (2%)
    ppermute x3, starting transfers between devices, local(): after = lax.ppermute(theta_low, 'theta', ring(-1, sectors))  32.4 us
    ppermute x3, waiting for transfers between devices, hop(): return lax.ppermute(value, AXES, hop_pairs(by, sectors, blocks))  29.7 us
    ppermute x3, waiting for transfers between devices, spin(): moved = lax.ppermute(value, AXES, spin_pairs(by, sectors, blocks))  15.6 us
    ppermute x3, starting transfers between devices, hop(): return lax.ppermute(value, AXES, hop_pairs(by, sectors, blocks))  9.67 us
    pallas_call x3, Pallas kernels, advance(): pl.pallas_call(functools.partial(section_kernel, section, blocks, last),...  9.33 us
    ppermute x3, starting transfers between devices, spin(): moved = lax.ppermute(value, AXES, spin_pairs(by, sectors, blocks))  7.75 us
    ppermute x3, starting transfers between devices, local(): before = lax.ppermute(theta_high, 'theta', ring(1, sectors))  7.37 us
    ppermute x3, starting transfers between devices, local(): core_in = lax.ppermute(core_rim, 'axial', core_pairs(blocks))  5.76 us
  transfers between devices with their start and end apart: 15, of which 6 were waited for; matrix products, arithmetic and copies ran while one was open for 1% of the time, Pallas kernels for 0%

profile of v1, /device:TPU:40, one launch (start us, length us, event | category | flops | bytes accessed | tf_op | source)
XLA Modules:
  0.0 122.5 jit_solution(6155569991516719864)
XLA Ops:
  0.0 0.0 copy-start
  0.0 1.1 copy-done
  1.1 0.0 copy-start.1
  1.1 0.1 rims.1
  1.2 3.5 %collective-permute-start.81 = (f32[5,16,128]{2,1,0:T(8,128)S(1)}, f32[5,16,128]{2,1,0:T(8,128)S(1)}, u32[]{:S(2)}, u32[]{:S(2)}) collective-permute-start(f32[5,16,128]{2,1,0:T(8,128)S(1)} %get-tuple-element.238), channel_id=1, source_target_pairs={{0,8},{8,16},{16,24},{24,32},{32,40},{40,48},{48,56},{56,64},{64,7... | collective-permute-start | bytes 122888 | tf_op jit(solution)/shard_map/ppermute | solution.py:228
  4.7 0.0 copy-start.4
  4.8 16.1 %collective-permute-start.82 = (f32[5,16,128]{2,1,0:T(8,128)S(1)}, f32[5,16,128]{2,1,0:T(8,128)S(1)}, u32[]{:S(2)}, u32[]{:S(2)}) collective-permute-start(f32[5,16,128]{2,1,0:T(8,128)S(1)} %get-tuple-element.239), channel_id=1, source_target_pairs={{0,760},{8,0},{16,8},{24,16},{32,24},{40,32},{48,40},{56,48},{64,5... | collective-permute-start | bytes 122888 | tf_op jit(solution)/shard_map/ppermute | solution.py:229
  20.9 1.9 %collective-permute-start.83 = (f32[5,16,128]{2,1,0:T(8,128)S(1)}, f32[5,16,128]{2,1,0:T(8,128)S(1)}, u32[]{:S(2)}, u32[]{:S(2)}) collective-permute-start(f32[5,16,128]{2,1,0:T(8,128)S(1)} %get-tuple-element.240), channel_id=1, source_target_pairs={{0,1},{1,0},{2,3},{3,2},{4,5},{5,4},{6,7},{7,6},{8,9},{9,8},{10,11... | collective-permute-start | bytes 122888 | tf_op jit(solution)/shard_map/ppermute | solution.py:230
  22.8 0.0 copy-done.4
  22.8 0.7 fusion
  24.1 0.0 copy-start.3
  24.1 0.7 copy-done.3
  24.8 5.9 %conditional.6 = (f32[5,16,128]{2,1,0:T(8,128)S(1)}) conditional(s32[]{:T(128)} %clamp.19, (pred[]{:T(512)}, f32[5,16,128]{2,1,0:T(8,128)S(1)}) %tuple.257, f32[5,16,128]{2,1,0:T(8,128)S(1)} %get-tuple-element.241.refs_9_, (pred[]{:T(512)}, f32[5,16,128]{2,1,0:T(8,128)S(1)}) %tuple.257, (pred[]{:T(512)}, ...), branch_computations={%region_0.1_spmd, %region_1.2_spmd, %region_2.3_spmd, %region_3.4_... | conditional | flops 10240 | bytes 286769 | solution.py:213
  24.8 3.9 %collective-permute-start.73 = (f32[5,16,128]{2,1,0:T(8,128)S(1)}, f32[5,16,128]{2,1,0:T(8,128)S(1)}, u32[]{:S(2)}, u32[]{:S(2)}) collective-permute-start(f32[5,16,128]{2,1,0:T(8,128)S(1)} %get-tuple-element.209), channel_id=1, source_target_pairs={{3,11},{12,4},{11,19},{20,12},{19,27},{28,20},{27,35},{36,28},{35,... | collective-permute-start | bytes 122888 | tf_op jit(solution)/shard_map/cond/branch_2_fun/ppermute | solution.py:207
  28.7 2.0 %collective-permute-done.73 = f32[5,16,128]{2,1,0:T(8,128)S(1)} collective-permute-done((f32[5,16,128]{2,1,0:T(8,128)S(1)}, f32[5,16,128]{2,1,0:T(8,128)S(1)}, u32[]{:S(2)}, u32[]{:S(2)}) %collective-permute-start.73) | collective-permute-done | bytes 40992 | tf_op jit(solution)/shard_map/cond/branch_2_fun/ppermute | solution.py:207
  30.7 0.0 copy-start.2
  30.7 15.9 %conditional.7 = (f32[5,16,128]{2,1,0:T(8,128)}) conditional(s32[]{:T(128)} %clamp.18, f32[5,16,128]{2,1,0:T(8,128)S(1)} %get-tuple-element.255, f32[5,16,128]{2,1,0:T(8,128)S(1)} %get-tuple-element.255, f32[5,16,128]{2,1,0:T(8,128)S(1)} %get-tuple-element.255, f32[5,16,128]{2,1,0:T(8,128)S(1)} %get-tuple-element.255, ...), branch_computations={%region_4.5_spmd, %region_5.6_spmd, %region_6.7_spmd, %region_7.8_... | conditional | bytes 163888 | solution.py:214
  30.7 5.8 %collective-permute-start.5 = (f32[5,16,128]{2,1,0:T(8,128)S(1)}, f32[5,16,128]{2,1,0:T(8,128)}, u32[]{:S(2)}, u32[]{:S(2)}) collective-permute-start(f32[5,16,128]{2,1,0:T(8,128)S(1)} %param.9), channel_id=1, source_target_pairs={{1,2},{2,1},{9,10},{10,9},{17,18},{18,17},{25,26},{26,25},{33,34},... | collective-permute-start | bytes 122888 | tf_op jit(solution)/shard_map/cond/branch_5_fun/ppermute | solution.py:211
  36.6 10.1 %collective-permute-done.5 = f32[5,16,128]{2,1,0:T(8,128)} collective-permute-done((f32[5,16,128]{2,1,0:T(8,128)S(1)}, f32[5,16,128]{2,1,0:T(8,128)}, u32[]{:S(2)}, u32[]{:S(2)}) %collective-permute-start.5) | collective-permute-done | bytes 40992 | tf_op jit(solution)/shard_map/cond/branch_5_fun/ppermute | solution.py:211
  46.6 0.0 collective-permute-done.81.refs_5_
  46.6 0.0 collective-permute-done.82.refs_6_
  46.6 0.0 collective-permute-done.83.refs_7_
  46.6 0.0 copy-done.1
  46.6 0.0 copy-done.2
  46.6 2.8 %section.3 = (f32[5,16,16,128]{3,2,1,0:T(8,128)S(1)}, f32[5,16,128]{2,1,0:T(8,128)S(1)}, f32[5,16,128]{2,1,0:T(8,128)S(1)}, f32[5,16,128]{2,1,0:T(8,128)S(1)}, f32[5,16,128]{2,1,0:T(8,128)S(1)}) custom-call(s32[1]{0:T(128)} %bitcast.place.refs_0_, f32[3,5,5]{2,1,0:T(8,128)S(1)} %copy.7.refs_1_, f32[3,2,16,16]{3,2,1,0:T(8,128)S(1)} %copy-done.2, ...), custom_call_target="tpu_custom_call" | custom-call | tf_op jit(solution)/shard_map/section/pallas_call | solution.py:157
  49.5 1.9 %collective-permute-start.84 = (f32[5,16,128]{2,1,0:T(8,128)S(1)}, f32[5,16,128]{2,1,0:T(8,128)S(1)}, u32[]{:S(2)}, u32[]{:S(2)}) collective-permute-start(f32[5,16,128]{2,1,0:T(8,128)S(1)} %get-tuple-element.243), channel_id=1, source_target_pairs={{0,8},{8,16},{16,24},{24,32},{32,40},{40,48},{48,56},{56,64},{64,7... | collective-permute-start | bytes 122888 | tf_op jit(solution)/shard_map/ppermute | solution.py:228
  51.4 8.1 %collective-permute-start.85 = (f32[5,16,128]{2,1,0:T(8,128)S(1)}, f32[5,16,128]{2,1,0:T(8,128)S(1)}, u32[]{:S(2)}, u32[]{:S(2)}) collective-permute-start(f32[5,16,128]{2,1,0:T(8,128)S(1)} %get-tuple-element.244), channel_id=1, source_target_pairs={{0,760},{8,0},{16,8},{24,16},{32,24},{40,32},{48,40},{56,48},{64,5... | collective-permute-start | bytes 122888 | tf_op jit(solution)/shard_map/ppermute | solution.py:229
  59.5 1.9 %collective-permute-start.86 = (f32[5,16,128]{2,1,0:T(8,128)S(1)}, f32[5,16,128]{2,1,0:T(8,128)S(1)}, u32[]{:S(2)}, u32[]{:S(2)}) collective-permute-start(f32[5,16,128]{2,1,0:T(8,128)S(1)} %get-tuple-element.245), channel_id=1, source_target_pairs={{0,1},{1,0},{2,3},{3,2},{4,5},{5,4},{6,7},{7,6},{8,9},{9,8},{10,11... | collective-permute-start | bytes 122888 | tf_op jit(solution)/shard_map/ppermute | solution.py:230
  62.2 10.1 %conditional.8 = (f32[5,16,128]{2,1,0:T(8,128)S(1)}) conditional(s32[]{:T(128)} %clamp.21, (pred[]{:T(512)}, f32[5,16,128]{2,1,0:T(8,128)S(1)}) %tuple.258, f32[5,16,128]{2,1,0:T(8,128)S(1)} %get-tuple-element.246.refs_9_, (pred[]{:T(512)}, f32[5,16,128]{2,1,0:T(8,128)S(1)}) %tuple.258, (pred[]{:T(512)}, ...), branch_computations={%region_28.29_spmd, %region_29.30_spmd, %region_30.31_spmd, %regio... | conditional | flops 10240 | bytes 286769 | solution.py:213
  62.2 1.9 %collective-permute-start.75 = (f32[5,16,128]{2,1,0:T(8,128)S(1)}, f32[5,16,128]{2,1,0:T(8,128)S(1)}, u32[]{:S(2)}, u32[]{:S(2)}) collective-permute-start(f32[5,16,128]{2,1,0:T(8,128)S(1)} %get-tuple-element.213), channel_id=1, source_target_pairs={{3,763},{764,4},{11,3},{4,12},{19,11},{12,20},{27,19},{20,28},{35,... | collective-permute-start | bytes 122888 | tf_op jit(solution)/shard_map/cond/branch_0_fun/ppermute | solution.py:207
  64.1 8.2 %collective-permute-done.75 = f32[5,16,128]{2,1,0:T(8,128)S(1)} collective-permute-done((f32[5,16,128]{2,1,0:T(8,128)S(1)}, f32[5,16,128]{2,1,0:T(8,128)S(1)}, u32[]{:S(2)}, u32[]{:S(2)}) %collective-permute-start.75) | collective-permute-done | bytes 40992 | tf_op jit(solution)/shard_map/cond/branch_0_fun/ppermute | solution.py:207
  72.3 11.1 %conditional.9 = (f32[5,16,128]{2,1,0:T(8,128)}) conditional(s32[]{:T(128)} %clamp.20, f32[5,16,128]{2,1,0:T(8,128)S(1)} %get-tuple-element.257, f32[5,16,128]{2,1,0:T(8,128)S(1)} %get-tuple-element.257, f32[5,16,128]{2,1,0:T(8,128)S(1)} %get-tuple-element.257, f32[5,16,128]{2,1,0:T(8,128)S(1)} %get-tuple-element.257, ...), branch_computations={%region_32.33_spmd, %region_33.34_spmd, %region_34.35_spmd, %regio... | conditional | bytes 163888 | solution.py:214
  72.3 1.9 %collective-permute-start.33 = (f32[5,16,128]{2,1,0:T(8,128)S(1)}, f32[5,16,128]{2,1,0:T(8,128)}, u32[]{:S(2)}, u32[]{:S(2)}) collective-permute-start(f32[5,16,128]{2,1,0:T(8,128)S(1)} %param.41), channel_id=1, source_target_pairs={{1,2},{2,1},{9,10},{10,9},{17,18},{18,17},{25,26},{26,25},{33,34},... | collective-permute-start | bytes 122888 | tf_op jit(solution)/shard_map/cond/branch_9_fun/ppermute | solution.py:211
  74.3 9.2 %collective-permute-done.33 = f32[5,16,128]{2,1,0:T(8,128)} collective-permute-done((f32[5,16,128]{2,1,0:T(8,128)S(1)}, f32[5,16,128]{2,1,0:T(8,128)}, u32[]{:S(2)}, u32[]{:S(2)}) %collective-permute-start.33) | collective-permute-done | bytes 40992 | tf_op jit(solution)/shard_map/cond/branch_9_fun/ppermute | solution.py:211
  83.5 0.0 collective-permute-done.84.refs_5_
  83.5 0.0 collective-permute-done.85.refs_6_
  83.5 0.0 collective-permute-done.86.refs_7_
  83.5 2.9 %section.4 = (f32[5,16,16,128]{3,2,1,0:T(8,128)S(1)}, f32[5,16,128]{2,1,0:T(8,128)S(1)}, f32[5,16,128]{2,1,0:T(8,128)S(1)}, f32[5,16,128]{2,1,0:T(8,128)S(1)}, f32[5,16,128]{2,1,0:T(8,128)S(1)}) custom-call(s32[1]{0:T(128)} %bitcast.place.refs_0_, f32[3,5,5]{2,1,0:T(8,128)S(1)} %copy.7.refs_1_, f32[3,2,16,16]{3,2,1,0:T(8,128)S(1)} %copy-done.2, ...), custom_call_target="tpu_custom_call" | custom-call | tf_op jit(solution)/shard_map/section/pallas_call | solution.py:157
  86.4 1.9 %collective-permute-start.87 = (f32[5,16,128]{2,1,0:T(8,128)S(1)}, f32[5,16,128]{2,1,0:T(8,128)S(1)}, u32[]{:S(2)}, u32[]{:S(2)}) collective-permute-start(f32[5,16,128]{2,1,0:T(8,128)S(1)} %get-tuple-element.248), channel_id=1, source_target_pairs={{0,8},{8,16},{16,24},{24,32},{32,40},{40,48},{48,56},{56,64},{64,7... | collective-permute-start | bytes 122888 | tf_op jit(solution)/shard_map/ppermute | solution.py:228
  88.3 8.1 %collective-permute-start.88 = (f32[5,16,128]{2,1,0:T(8,128)S(1)}, f32[5,16,128]{2,1,0:T(8,128)S(1)}, u32[]{:S(2)}, u32[]{:S(2)}) collective-permute-start(f32[5,16,128]{2,1,0:T(8,128)S(1)} %get-tuple-element.249), channel_id=1, source_target_pairs={{0,760},{8,0},{16,8},{24,16},{32,24},{40,32},{48,40},{56,48},{64,5... | collective-permute-start | bytes 122888 | tf_op jit(solution)/shard_map/ppermute | solution.py:229
  96.4 1.9 %collective-permute-start.89 = (f32[5,16,128]{2,1,0:T(8,128)S(1)}, f32[5,16,128]{2,1,0:T(8,128)S(1)}, u32[]{:S(2)}, u32[]{:S(2)}) collective-permute-start(f32[5,16,128]{2,1,0:T(8,128)S(1)} %get-tuple-element.250), channel_id=1, source_target_pairs={{0,1},{1,0},{2,3},{3,2},{4,5},{5,4},{6,7},{7,6},{8,9},{9,8},{10,11... | collective-permute-start | bytes 122888 | tf_op jit(solution)/shard_map/ppermute | solution.py:230
  99.1 7.4 %conditional.10 = (f32[5,16,128]{2,1,0:T(8,128)S(1)}) conditional(s32[]{:T(128)} %clamp.23, (pred[]{:T(512)}, f32[5,16,128]{2,1,0:T(8,128)S(1)}) %tuple.259, f32[5,16,128]{2,1,0:T(8,128)S(1)} %get-tuple-element.251.refs_9_, (pred[]{:T(512)}, f32[5,16,128]{2,1,0:T(8,128)S(1)}) %tuple.259, (pred[]{:T(512)}, ...), branch_computations={%region_56.57_spmd, %region_57.58_spmd, %region_58.59_spmd, %regio... | conditional | flops 10240 | bytes 286769 | solution.py:213
  99.1 1.9 %collective-permute-start.80 = (f32[5,16,128]{2,1,0:T(8,128)S(1)}, f32[5,16,128]{2,1,0:T(8,128)S(1)}, u32[]{:S(2)}, u32[]{:S(2)}) collective-permute-start(f32[5,16,128]{2,1,0:T(8,128)S(1)} %get-tuple-element.223), channel_id=1, source_target_pairs={{3,19},{20,4},{11,27},{28,12},{19,35},{36,20},{27,43},{44,28},{35,... | collective-permute-start | bytes 122888 | tf_op jit(solution)/shard_map/cond/branch_3_fun/ppermute | solution.py:207
  101.0 5.5 %collective-permute-done.80 = f32[5,16,128]{2,1,0:T(8,128)S(1)} collective-permute-done((f32[5,16,128]{2,1,0:T(8,128)S(1)}, f32[5,16,128]{2,1,0:T(8,128)S(1)}, u32[]{:S(2)}, u32[]{:S(2)}) %collective-permute-start.80) | collective-permute-done | bytes 40992 | tf_op jit(solution)/shard_map/cond/branch_3_fun/ppermute | solution.py:207
  106.5 12.3 %conditional.11 = (f32[5,16,128]{2,1,0:T(8,128)}) conditional(s32[]{:T(128)} %clamp.22, f32[5,16,128]{2,1,0:T(8,128)S(1)} %get-tuple-element.259, f32[5,16,128]{2,1,0:T(8,128)S(1)} %get-tuple-element.259, f32[5,16,128]{2,1,0:T(8,128)S(1)} %get-tuple-element.259, f32[5,16,128]{2,1,0:T(8,128)S(1)} %get-tuple-element.259, ...), branch_computations={%region_60.61_spmd, %region_61.62_spmd, %region_62.63_spmd, %regio... | conditional | bytes 163888 | solution.py:214
  106.5 1.9 %collective-permute-start.64 = (f32[5,16,128]{2,1,0:T(8,128)S(1)}, f32[5,16,128]{2,1,0:T(8,128)}, u32[]{:S(2)}, u32[]{:S(2)}) collective-permute-start(f32[5,16,128]{2,1,0:T(8,128)S(1)} %param.76), channel_id=1, source_target_pairs={{1,2},{2,1},{9,10},{10,9},{17,18},{18,17},{25,26},{26,25},{33,34},... | collective-permute-start | bytes 122888 | tf_op jit(solution)/shard_map/cond/branch_16_fun/ppermute | solution.py:211
  108.4 10.4 %collective-permute-done.64 = f32[5,16,128]{2,1,0:T(8,128)} collective-permute-done((f32[5,16,128]{2,1,0:T(8,128)S(1)}, f32[5,16,128]{2,1,0:T(8,128)}, u32[]{:S(2)}, u32[]{:S(2)}) %collective-permute-start.64) | collective-permute-done | bytes 40992 | tf_op jit(solution)/shard_map/cond/branch_16_fun/ppermute | solution.py:211
  118.8 0.0 collective-permute-done.87.refs_5_
  118.8 0.0 collective-permute-done.88.refs_6_
  118.8 0.0 collective-permute-done.89.refs_7_
  118.8 3.7 %section.5 = f32[5,16,16,128]{3,2,1,0:T(8,128)} custom-call(s32[1]{0:T(128)} %bitcast.place.refs_0_, f32[3,5,5]{2,1,0:T(8,128)S(1)} %copy.7.refs_1_, f32[3,2,16,16]{3,2,1,0:T(8,128)S(1)} %copy-done.2, f32[5,16,16,128]{3,2,1,0:T(8,128)S(1)} %get-tuple-element.247.refs_3_, f32[5,16,16,128]{3,2,1,0:T(8,128)S(1)} %copy-done.1, ...), custom_call_target="tpu_custom_call" | custom-call | tf_op jit(solution)/shard_map/section/pallas_call | solution.py:157
  (4 shorter events, 0.0 us)
Async XLA Ops:
  0.0 1.1 copy-start
  1.1 45.5 %copy-start.1 = (f32[5,16,16,128]{3,2,1,0:T(8,128)S(1)}, f32[5,16,16,128]{3,2,1,0:T(8,128)}, u32[]{:S(2)}) copy-start(f32[5,16,16,128]{3,2,1,0:T(8,128)} %refs_4_.5) | copy-start | bytes 1966084
  1.2 45.4 %collective-permute-start.81 = (f32[5,16,128]{2,1,0:T(8,128)S(1)}, f32[5,16,128]{2,1,0:T(8,128)S(1)}, u32[]{:S(2)}, u32[]{:S(2)}) collective-permute-start(f32[5,16,128]{2,1,0:T(8,128)S(1)} %get-tuple-element.238), channel_id=1, source_target_pairs={{0,8},{8,16},{16,24},{24,32},{32,40},{40,48},{48,56},{56,64},{64,7... | collective-permute-start | bytes 122888 | tf_op jit(solution)/shard_map/ppermute | solution.py:228
  4.7 18.0 %copy-start.4 = (s32[3]{0:T(128)S(1)}, s32[3]{0:T(128)}, u32[]{:S(2)}) copy-start(s32[3]{0:T(128)} %param.91) | copy-start | bytes 40
  4.8 41.9 %collective-permute-start.82 = (f32[5,16,128]{2,1,0:T(8,128)S(1)}, f32[5,16,128]{2,1,0:T(8,128)S(1)}, u32[]{:S(2)}, u32[]{:S(2)}) collective-permute-start(f32[5,16,128]{2,1,0:T(8,128)S(1)} %get-tuple-element.239), channel_id=1, source_target_pairs={{0,760},{8,0},{16,8},{24,16},{32,24},{40,32},{48,40},{56,48},{64,5... | collective-permute-start | bytes 122888 | tf_op jit(solution)/shard_map/ppermute | solution.py:229
  20.9 25.8 %collective-permute-start.83 = (f32[5,16,128]{2,1,0:T(8,128)S(1)}, f32[5,16,128]{2,1,0:T(8,128)S(1)}, u32[]{:S(2)}, u32[]{:S(2)}) collective-permute-start(f32[5,16,128]{2,1,0:T(8,128)S(1)} %get-tuple-element.240), channel_id=1, source_target_pairs={{0,1},{1,0},{2,3},{3,2},{4,5},{5,4},{6,7},{7,6},{8,9},{9,8},{10,11... | collective-permute-start | bytes 122888 | tf_op jit(solution)/shard_map/ppermute | solution.py:230
  24.1 0.7 copy-start.3
  24.8 5.9 %collective-permute-start.73 = (f32[5,16,128]{2,1,0:T(8,128)S(1)}, f32[5,16,128]{2,1,0:T(8,128)S(1)}, u32[]{:S(2)}, u32[]{:S(2)}) collective-permute-start(f32[5,16,128]{2,1,0:T(8,128)S(1)} %get-tuple-element.209), channel_id=1, source_target_pairs={{3,11},{12,4},{11,19},{20,12},{19,27},{28,20},{27,35},{36,28},{35,... | collective-permute-start | bytes 122888 | tf_op jit(solution)/shard_map/cond/branch_2_fun/ppermute | solution.py:207
  30.7 16.0 %copy-start.2 = (f32[3,2,16,16]{3,2,1,0:T(8,128)S(1)}, f32[3,2,16,16]{3,2,1,0:T(8,128)}, u32[]{:S(2)}) copy-start(f32[3,2,16,16]{3,2,1,0:T(8,128)} %refs_2_.5) | copy-start | bytes 18436
  30.7 15.9 %collective-permute-start.5 = (f32[5,16,128]{2,1,0:T(8,128)S(1)}, f32[5,16,128]{2,1,0:T(8,128)}, u32[]{:S(2)}, u32[]{:S(2)}) collective-permute-start(f32[5,16,128]{2,1,0:T(8,128)S(1)} %param.9), channel_id=1, source_target_pairs={{1,2},{2,1},{9,10},{10,9},{17,18},{18,17},{25,26},{26,25},{33,34},... | collective-permute-start | bytes 122888 | tf_op jit(solution)/shard_map/cond/branch_5_fun/ppermute | solution.py:211
  49.5 34.0 %collective-permute-start.84 = (f32[5,16,128]{2,1,0:T(8,128)S(1)}, f32[5,16,128]{2,1,0:T(8,128)S(1)}, u32[]{:S(2)}, u32[]{:S(2)}) collective-permute-start(f32[5,16,128]{2,1,0:T(8,128)S(1)} %get-tuple-element.243), channel_id=1, source_target_pairs={{0,8},{8,16},{16,24},{24,32},{32,40},{40,48},{48,56},{56,64},{64,7... | collective-permute-start | bytes 122888 | tf_op jit(solution)/shard_map/ppermute | solution.py:228
  51.4 32.1 %collective-permute-start.85 = (f32[5,16,128]{2,1,0:T(8,128)S(1)}, f32[5,16,128]{2,1,0:T(8,128)S(1)}, u32[]{:S(2)}, u32[]{:S(2)}) collective-permute-start(f32[5,16,128]{2,1,0:T(8,128)S(1)} %get-tuple-element.244), channel_id=1, source_target_pairs={{0,760},{8,0},{16,8},{24,16},{32,24},{40,32},{48,40},{56,48},{64,5... | collective-permute-start | bytes 122888 | tf_op jit(solution)/shard_map/ppermute | solution.py:229
  59.5 23.9 %collective-permute-start.86 = (f32[5,16,128]{2,1,0:T(8,128)S(1)}, f32[5,16,128]{2,1,0:T(8,128)S(1)}, u32[]{:S(2)}, u32[]{:S(2)}) collective-permute-start(f32[5,16,128]{2,1,0:T(8,128)S(1)} %get-tuple-element.245), channel_id=1, source_target_pairs={{0,1},{1,0},{2,3},{3,2},{4,5},{5,4},{6,7},{7,6},{8,9},{9,8},{10,11... | collective-permute-start | bytes 122888 | tf_op jit(solution)/shard_map/ppermute | solution.py:230
  62.2 10.1 %collective-permute-start.75 = (f32[5,16,128]{2,1,0:T(8,128)S(1)}, f32[5,16,128]{2,1,0:T(8,128)S(1)}, u32[]{:S(2)}, u32[]{:S(2)}) collective-permute-start(f32[5,16,128]{2,1,0:T(8,128)S(1)} %get-tuple-element.213), channel_id=1, source_target_pairs={{3,763},{764,4},{11,3},{4,12},{19,11},{12,20},{27,19},{20,28},{35,... | collective-permute-start | bytes 122888 | tf_op jit(solution)/shard_map/cond/branch_0_fun/ppermute | solution.py:207
  72.3 11.1 %collective-permute-start.33 = (f32[5,16,128]{2,1,0:T(8,128)S(1)}, f32[5,16,128]{2,1,0:T(8,128)}, u32[]{:S(2)}, u32[]{:S(2)}) collective-permute-start(f32[5,16,128]{2,1,0:T(8,128)S(1)} %param.41), channel_id=1, source_target_pairs={{1,2},{2,1},{9,10},{10,9},{17,18},{18,17},{25,26},{26,25},{33,34},... | collective-permute-start | bytes 122888 | tf_op jit(solution)/shard_map/cond/branch_9_fun/ppermute | solution.py:211
  86.4 32.5 %collective-permute-start.87 = (f32[5,16,128]{2,1,0:T(8,128)S(1)}, f32[5,16,128]{2,1,0:T(8,128)S(1)}, u32[]{:S(2)}, u32[]{:S(2)}) collective-permute-start(f32[5,16,128]{2,1,0:T(8,128)S(1)} %get-tuple-element.248), channel_id=1, source_target_pairs={{0,8},{8,16},{16,24},{24,32},{32,40},{40,48},{48,56},{56,64},{64,7... | collective-permute-start | bytes 122888 | tf_op jit(solution)/shard_map/ppermute | solution.py:228
  88.3 30.6 %collective-permute-start.88 = (f32[5,16,128]{2,1,0:T(8,128)S(1)}, f32[5,16,128]{2,1,0:T(8,128)S(1)}, u32[]{:S(2)}, u32[]{:S(2)}) collective-permute-start(f32[5,16,128]{2,1,0:T(8,128)S(1)} %get-tuple-element.249), channel_id=1, source_target_pairs={{0,760},{8,0},{16,8},{24,16},{32,24},{40,32},{48,40},{56,48},{64,5... | collective-permute-start | bytes 122888 | tf_op jit(solution)/shard_map/ppermute | solution.py:229
  96.4 22.4 %collective-permute-start.89 = (f32[5,16,128]{2,1,0:T(8,128)S(1)}, f32[5,16,128]{2,1,0:T(8,128)S(1)}, u32[]{:S(2)}, u32[]{:S(2)}) collective-permute-start(f32[5,16,128]{2,1,0:T(8,128)S(1)} %get-tuple-element.250), channel_id=1, source_target_pairs={{0,1},{1,0},{2,3},{3,2},{4,5},{5,4},{6,7},{7,6},{8,9},{9,8},{10,11... | collective-permute-start | bytes 122888 | tf_op jit(solution)/shard_map/ppermute | solution.py:230
  99.1 7.4 %collective-permute-start.80 = (f32[5,16,128]{2,1,0:T(8,128)S(1)}, f32[5,16,128]{2,1,0:T(8,128)S(1)}, u32[]{:S(2)}, u32[]{:S(2)}) collective-permute-start(f32[5,16,128]{2,1,0:T(8,128)S(1)} %get-tuple-element.223), channel_id=1, source_target_pairs={{3,19},{20,4},{11,27},{28,12},{19,35},{36,20},{27,43},{44,28},{35,... | collective-permute-start | bytes 122888 | tf_op jit(solution)/shard_map/cond/branch_3_fun/ppermute | solution.py:207
  106.5 12.3 %collective-permute-start.64 = (f32[5,16,128]{2,1,0:T(8,128)S(1)}, f32[5,16,128]{2,1,0:T(8,128)}, u32[]{:S(2)}, u32[]{:S(2)}) collective-permute-start(f32[5,16,128]{2,1,0:T(8,128)S(1)} %param.76), channel_id=1, source_target_pairs={{1,2},{2,1},{9,10},{10,9},{17,18},{18,17},{25,26},{26,25},{33,34},... | collective-permute-start | bytes 122888 | tf_op jit(solution)/shard_map/cond/branch_16_fun/ppermute | solution.py:211

commit v2 on v1

--- a/solution.py
+++ b/solution.py
@@ -20,31 +20,27 @@
 SMEM = pl.BlockSpec(memory_space=pltpu.SMEM)
 
 
-def write_rims(value_of, is_odd, theta_low, theta_high, core_rim, hop_rim, cells):
+def write_axial_rims(value, v, t, is_odd, low_rim, high_rim, core_rim):
+    first, last = value[:1], value[-1:]
+    core_rim[v, pl.ds(t, 1), :] = jnp.where(is_odd, first, last)
+    hop = jnp.where(is_odd, last, first)
+    low_rim[NVAR + v, pl.ds(t, 1), :] = hop
+    high_rim[NVAR + v, pl.ds(t, 1), :] = hop
+
+
+def rims_kernel(place, current, low_rim, high_rim, core_rim):
+    is_odd = place[0] % 2 == 1
+    cells = current.shape[1]
     for v in range(NVAR):
-        theta_low[v] = value_of(v, 0)
-        theta_high[v] = value_of(v, cells - 1)
+        low_rim[v] = current[v, 0]
+        high_rim[v] = current[v, cells - 1]
 
     def step(t, carry):
         for v in range(NVAR):
-            write_axial_rims(value_of(v, t), v, t, is_odd, core_rim, hop_rim)
+            write_axial_rims(current[v, t], v, t, is_odd, low_rim, high_rim, core_rim)
         return carry
 
     lax.fori_loop(0, cells, step, 0)
-
-
-def write_axial_rims(value, v, t, is_odd, core_rim, hop_rim):
-    first, last = value[:1], value[-1:]
-    core_rim[v, pl.ds(t, 1), :] = jnp.where(is_odd, first, last)
-    hop_rim[v, pl.ds(t, 1), :] = jnp.where(is_odd, last, first)
-
-
-def rims_kernel(place, current, theta_low, theta_high, core_rim, hop_rim):
-    is_odd = place[0] % 2 == 1
-    cells = current.shape[1]
-    write_rims(
-        lambda v, t: current[v, t], is_odd, theta_low, theta_high, core_rim, hop_rim, cells
-    )
 
 
 def section_kernel(section, blocks, last, *refs):
@@ -72,7 +68,7 @@
 
         @pl.when(at_end)
         def _():
-            hop_side[...] = hop_own[...]
+            hop_side[...] = hop_own[NVAR:]
 
         @pl.when(inside)
         def _():
@@ -116,7 +112,7 @@
             new = smooth[v] - (0.5 * push) * slope[v]
             out[v, t] = new
             if not last:
-                write_axial_rims(new, v, t, is_odd, rims[2], rims[3])
+                write_axial_rims(new, v, t, is_odd, *rims)
 
     def step(t, carry):
         cell_row(t, lambda w: current[w, t - 1], lambda w: current[w, t + 1])
@@ -133,9 +129,9 @@
 
 def rim_shapes(current):
     nvar, cells, width, radial = current.shape
-    theta_rim = jax.ShapeDtypeStruct((nvar, width, radial), jnp.float32)
+    theta_rim = jax.ShapeDtypeStruct((2 * nvar, width, radial), jnp.float32)
     axial_rim = jax.ShapeDtypeStruct((nvar, cells, radial), jnp.float32)
-    return (theta_rim, theta_rim, axial_rim, axial_rim)
+    return (theta_rim, theta_rim, axial_rim)
 
 
 def first_rims(place, current):
@@ -143,7 +139,7 @@
         rims_kernel,
         out_shape=rim_shapes(current),
         in_specs=[SMEM, VMEM],
-        out_specs=(VMEM,) * 4,
+        out_specs=(VMEM,) * 3,
         compiler_params=pltpu.CompilerParams(vmem_limit_bytes=8 << 20),
         name="rims",
     )(place, current)
@@ -173,19 +169,6 @@
     return [(a, a ^ 1) for a in range(blocks)]
 
 
-FINE = 4
-
-
-def spin_pairs(by, sectors, blocks):
-    rotor, stator = blocks // 2 - 1, blocks // 2
-    pairs = []
-    for t in range(sectors):
-        ahead = (t + by) % sectors
-        pairs.append((t * blocks + rotor, ahead * blocks + rotor))
-        pairs.append((ahead * blocks + stator, t * blocks + stator))
-    return pairs
-
-
 def hop_pairs(by, sectors, blocks):
     pairs = []
     for a in range(1, blocks - 1, 2):
@@ -196,39 +179,39 @@
     return pairs
 
 
-def exchange_hop(face, offset, at_plane, sectors, blocks):
-    shifts = list(range(-1, FINE - 1))
-    fine = (offset + 1) % FINE
-    coarse = (offset + 1) // FINE % (sectors // FINE)
-
-    def spin(by, value):
-        if by == 0:
-            return value
-        moved = lax.ppermute(value, AXES, spin_pairs(by, sectors, blocks))
-        return jnp.where(at_plane, moved, value)
+def exchange_hop(own, before, after, offset, side, sectors, blocks):
+    fine = (offset + 1) % 3 - 1
+    coarse = (offset + 1) // 3 % (sectors // 3)
+    turn = fine * side
+    face = jnp.where(turn == 1, before, jnp.where(turn == -1, after, own))
 
     def hop(by, value):
         return lax.ppermute(value, AXES, hop_pairs(by, sectors, blocks))
 
-    face = lax.switch(fine, [functools.partial(spin, by) for by in shifts], face)
-    return lax.switch(
-        coarse, [functools.partial(hop, FINE * k) for k in range(sectors // FINE)], face
-    )
+    return lax.switch(coarse, [functools.partial(hop, 3 * k) for k in range(sectors // 3)], face)
 
 
 def local(conserved, flux_matrices, slide_weights, rotor_offsets):
     sectors, blocks = lax.axis_size("theta"), lax.axis_size("axial")
     index = lax.axis_index("axial")
     place = jnp.full((1,), index, jnp.int32)
-    at_plane = (index == blocks // 2) | (index == blocks // 2 - 1)
+    side = jnp.where(index == blocks // 2 - 1, 1, jnp.where(index == blocks // 2, -1, 0))
     current, rims = conserved, first_rims(place, conserved)
     sections = len(SECTION_WEIGHTS)
     for section in range(sections):
-        theta_low, theta_high, core_rim, hop_rim = rims
-        before = lax.ppermute(theta_high, "theta", ring(1, sectors))
-        after = lax.ppermute(theta_low, "theta", ring(-1, sectors))
+        low_rim, high_rim, core_rim = rims
+        before = lax.ppermute(high_rim, "theta", ring(1, sectors))
+        after = lax.ppermute(low_rim, "theta", ring(-1, sectors))
         core_in = lax.ppermute(core_rim, "axial", core_pairs(blocks))
-        hop_in = exchange_hop(hop_rim, rotor_offsets[section], at_plane, sectors, blocks)
+        hop_in = exchange_hop(
+            low_rim[NVAR:],
+            before[NVAR:],
+            after[NVAR:],
+            rotor_offsets[section],
+            side,
+            sectors,
+            blocks,
+        )
         current, *rims = advance(
             section,
             blocks,
@@ -238,7 +221,7 @@
             slide_weights,
             current,
             conserved,
-            (before, after, core_in, hop_in, hop_rim),
+            (before, after, core_in, hop_in, low_rim),
         )
     return current
 

time: 123 us -> 100 us (0.81)
  starting transfers between devices: 62.9 us -> 47.6 us
  waiting for transfers between devices: 45.3 us -> 37.6 us
    ppermute x9 -> x6, starting transfers between devices: 47.5 us -> 35.5 us  [the longest x3 27.8 us: local(): after = lax.ppermute(low_rim, 'theta', ring(-1, sectors))]
    ppermute x9 -> x6, waiting for transfers between devices: 15.6 us -> 8.75 us  [the longest x3 8.75 us: local(): before = lax.ppermute(high_rim, 'theta', ring(1, sectors))]
    ppermute x3, starting transfers between devices: 9.67 us -> 6.36 us  [hop(): return lax.ppermute(value, AXES, hop_pairs(by, sectors, blocks))]
  transfers between devices with their start and end apart: 15 -> 12, of which waited for: 6 -> 5; matrix products, arithmetic and copies ran while one was open for 1% -> 1% of each run, Pallas kernels for 0% -> 0%
where the time goes in v2:
time: 100 us; the launch traced here: 99.4 us
  starting transfers between devices  47.6 us (48%)
  waiting for transfers between devices  37.6 us (38%)
  Pallas kernels  9.47 us (9%)
  local copies, waits for them, and re-layouts  2.43 us (2%)
  between operations  2.16 us (2%)
    ppermute x3, waiting for transfers between devices, hop(): return lax.ppermute(value, AXES, hop_pairs(by, sectors, blocks))  28.8 us
    ppermute x3, starting transfers between devices, local(): after = lax.ppermute(low_rim, 'theta', ring(-1, sectors))  27.8 us
    pallas_call x3, Pallas kernels, advance(): pl.pallas_call(functools.partial(section_kernel, section, blocks, last),...  9.34 us
    ppermute x3, waiting for transfers between devices, local(): before = lax.ppermute(high_rim, 'theta', ring(1, sectors))  8.75 us
    ppermute x3, starting transfers between devices, local(): before = lax.ppermute(high_rim, 'theta', ring(1, sectors))  7.76 us
    ppermute x3, starting transfers between devices, hop(): return lax.ppermute(value, AXES, hop_pairs(by, sectors, blocks))  6.36 us
    ppermute x3, starting transfers between devices, local(): core_in = lax.ppermute(core_rim, 'axial', core_pairs(blocks))  5.76 us
  transfers between devices with their start and end apart: 12, of which 5 were waited for; matrix products, arithmetic and copies ran while one was open for 1% of the time, Pallas kernels for 0%

profile of v2, /device:TPU:40, one launch (start us, length us, event | category | flops | bytes accessed | tf_op | source)
XLA Modules:
  0.0 99.4 jit_solution(7024429982024341055)
XLA Ops:
  0.0 0.0 copy-start
  0.0 1.1 %copy-done = f32[5,16,16,128]{3,2,1,0:T(8,128)S(1)} copy-done((f32[5,16,16,128]{3,2,1,0:T(8,128)S(1)}, f32[5,16,16,128]{3,2,1,0:T(8,128)}, u32[]{:S(2)}) %copy-start) | copy-done | bytes 655384
  1.1 0.0 copy-start.1
  1.1 0.1 rims.1
  1.2 17.7 %collective-permute-start.97 = (f32[10,16,128]{2,1,0:T(8,128)S(1)}, f32[10,16,128]{2,1,0:T(8,128)S(1)}, u32[]{:S(2)}, u32[]{:S(2)}) collective-permute-start(f32[10,16,128]{2,1,0:T(8,128)S(1)} %get-tuple-element.212.refs_9_), channel_id=1, source_target_pairs={{0,760},{8,0},{16,8},{24,16},{32,24},{40,32},{48,40},{56,48},{64,5... | collective-permute-start | bytes 245768 | tf_op jit(solution)/shard_map/ppermute | solution.py:204
  18.9 0.0 copy-start.4
  18.9 1.9 %collective-permute-start.96 = (f32[10,16,128]{2,1,0:T(8,128)S(1)}, f32[10,16,128]{2,1,0:T(8,128)S(1)}, u32[]{:S(2)}, u32[]{:S(2)}) collective-permute-start(f32[10,16,128]{2,1,0:T(8,128)S(1)} %get-tuple-element.211), channel_id=1, source_target_pairs={{0,8},{8,16},{16,24},{24,32},{32,40},{40,48},{48,56},{56,64},{64,7... | collective-permute-start | bytes 245768 | tf_op jit(solution)/shard_map/ppermute | solution.py:203
  20.9 1.9 %collective-permute-start.98 = (f32[5,16,128]{2,1,0:T(8,128)S(1)}, f32[5,16,128]{2,1,0:T(8,128)S(1)}, u32[]{:S(2)}, u32[]{:S(2)}) collective-permute-start(f32[5,16,128]{2,1,0:T(8,128)S(1)} %get-tuple-element.213), channel_id=1, source_target_pairs={{0,1},{1,0},{2,3},{3,2},{4,5},{5,4},{6,7},{7,6},{8,9},{9,8},{10,11... | collective-permute-start | bytes 122888 | tf_op jit(solution)/shard_map/ppermute | solution.py:205
  22.8 0.0 copy-done.4
  22.8 0.7 fusion.3
  24.1 0.0 copy-start.3
  24.1 0.7 copy-done.3
  24.8 0.0 collective-permute-done.97.refs_6_
  24.8 4.7 %collective-permute-done.96.refs_5_ = f32[10,16,128]{2,1,0:T(8,128)S(1)} collective-permute-done((f32[10,16,128]{2,1,0:T(8,128)S(1)}, f32[10,16,128]{2,1,0:T(8,128)S(1)}, u32[]{:S(2)}, u32[]{:S(2)}) %collective-permute-start.96) | collective-permute-done | bytes 81952 | tf_op jit(solution)/shard_map/ppermute | solution.py:203
  29.5 0.0 copy-start.2
  29.5 13.9 %conditional.3 = (f32[5,16,128]{2,1,0:T(8,128)}) conditional(s32[]{:T(128)} %clamp.9, f32[5,16,128]{2,1,0:T(8,128)S(1)} %fusion.2, f32[5,16,128]{2,1,0:T(8,128)S(1)} %fusion.2, f32[5,16,128]{2,1,0:T(8,128)S(1)} %fusion.2, f32[5,16,128]{2,1,0:T(8,128)S(1)} %fusion.2, f32[5,16,128]{2,1,0:T(8,128)S(1)} %fusion.2, ...), branch_computations={%region_0.1_spmd, %region_1.2_spmd, %region_2.3_spmd, %region_3.4_... | conditional | bytes 163888 | solution.py:191
  29.5 1.9 %collective-permute-start.2 = (f32[5,16,128]{2,1,0:T(8,128)S(1)}, f32[5,16,128]{2,1,0:T(8,128)}, u32[]{:S(2)}, u32[]{:S(2)}) collective-permute-start(f32[5,16,128]{2,1,0:T(8,128)S(1)} %param.2), channel_id=1, source_target_pairs={{1,2},{2,1},{9,10},{10,9},{17,18},{18,17},{25,26},{26,25},{33,34},... | collective-permute-start | bytes 122888 | tf_op jit(solution)/shard_map/cond/branch_2_fun/ppermute | solution.py:189
  31.5 11.9 %collective-permute-done.2 = f32[5,16,128]{2,1,0:T(8,128)} collective-permute-done((f32[5,16,128]{2,1,0:T(8,128)S(1)}, f32[5,16,128]{2,1,0:T(8,128)}, u32[]{:S(2)}, u32[]{:S(2)}) %collective-permute-start.2) | collective-permute-done | bytes 40992 | tf_op jit(solution)/shard_map/cond/branch_2_fun/ppermute | solution.py:189
  43.4 0.0 collective-permute-done.98.refs_7_
  43.4 0.0 copy-done.1
  43.4 0.0 copy-done.2
  43.4 2.8 %section.3 = (f32[5,16,16,128]{3,2,1,0:T(8,128)S(1)}, f32[10,16,128]{2,1,0:T(8,128)S(1)}, f32[10,16,128]{2,1,0:T(8,128)S(1)}, f32[5,16,128]{2,1,0:T(8,128)S(1)}) custom-call(s32[1]{0:T(128)} %bitcast.place.refs_0_, f32[3,5,5]{2,1,0:T(8,128)S(1)} %copy.7.refs_1_, f32[3,2,16,16]{3,2,1,0:T(8,128)S(1)} %copy-done.2, f32[5,16,16,128]{3,2,1,0:T(8,128)S(1)} %copy-done.1, ...), custom_call_target="tpu_custom_call" | custom-call | tf_op jit(solution)/shard_map/section/pallas_call | solution.py:153
  46.2 1.9 %collective-permute-start.100 = (f32[10,16,128]{2,1,0:T(8,128)S(1)}, f32[10,16,128]{2,1,0:T(8,128)S(1)}, u32[]{:S(2)}, u32[]{:S(2)}) collective-permute-start(f32[10,16,128]{2,1,0:T(8,128)S(1)} %get-tuple-element.216.refs_9_), channel_id=1, source_target_pairs={{0,760},{8,0},{16,8},{24,16},{32,24},{40,32},{48,40},{56,48},{64,5... | collective-permute-start | bytes 245768 | tf_op jit(solution)/shard_map/ppermute | solution.py:204
  48.2 3.9 %collective-permute-start.99 = (f32[10,16,128]{2,1,0:T(8,128)S(1)}, f32[10,16,128]{2,1,0:T(8,128)S(1)}, u32[]{:S(2)}, u32[]{:S(2)}) collective-permute-start(f32[10,16,128]{2,1,0:T(8,128)S(1)} %get-tuple-element.215), channel_id=1, source_target_pairs={{0,8},{8,16},{16,24},{24,32},{32,40},{40,48},{48,56},{56,64},{64,7... | collective-permute-start | bytes 245768 | tf_op jit(solution)/shard_map/ppermute | solution.py:203
  52.8 1.9 %collective-permute-start.101 = (f32[5,16,128]{2,1,0:T(8,128)S(1)}, f32[5,16,128]{2,1,0:T(8,128)S(1)}, u32[]{:S(2)}, u32[]{:S(2)}) collective-permute-start(f32[5,16,128]{2,1,0:T(8,128)S(1)} %get-tuple-element.217), channel_id=1, source_target_pairs={{0,1},{1,0},{2,3},{3,2},{4,5},{5,4},{6,7},{7,6},{8,9},{9,8},{10,11... | collective-permute-start | bytes 122888 | tf_op jit(solution)/shard_map/ppermute | solution.py:205
  54.7 0.0 collective-permute-done.100.refs_6_
  54.7 4.0 %collective-permute-done.99.refs_5_ = f32[10,16,128]{2,1,0:T(8,128)S(1)} collective-permute-done((f32[10,16,128]{2,1,0:T(8,128)S(1)}, f32[10,16,128]{2,1,0:T(8,128)S(1)}, u32[]{:S(2)}, u32[]{:S(2)}) %collective-permute-start.99) | collective-permute-done | bytes 81952 | tf_op jit(solution)/shard_map/ppermute | solution.py:203
  58.7 7.6 %conditional.4 = (f32[5,16,128]{2,1,0:T(8,128)}) conditional(s32[]{:T(128)} %clamp.10, f32[5,16,128]{2,1,0:T(8,128)S(1)} %fusion.1, f32[5,16,128]{2,1,0:T(8,128)S(1)} %fusion.1, f32[5,16,128]{2,1,0:T(8,128)S(1)} %fusion.1, f32[5,16,128]{2,1,0:T(8,128)S(1)} %fusion.1, f32[5,16,128]{2,1,0:T(8,128)S(1)} %fusion.1, ...), branch_computations={%region_32.33_spmd, %region_33.34_spmd, %region_34.35_spmd, %regio... | conditional | bytes 163888 | solution.py:191
  58.8 2.5 %collective-permute-start.32 = (f32[5,16,128]{2,1,0:T(8,128)S(1)}, f32[5,16,128]{2,1,0:T(8,128)}, u32[]{:S(2)}, u32[]{:S(2)}) collective-permute-start(f32[5,16,128]{2,1,0:T(8,128)S(1)} %param.32), channel_id=1, source_target_pairs={{1,2},{2,1},{9,10},{10,9},{17,18},{18,17},{25,26},{26,25},{33,34},... | collective-permute-start | bytes 122888 | tf_op jit(solution)/shard_map/cond/branch_0_fun/ppermute | solution.py:189
  61.3 5.0 %collective-permute-done.32 = f32[5,16,128]{2,1,0:T(8,128)} collective-permute-done((f32[5,16,128]{2,1,0:T(8,128)S(1)}, f32[5,16,128]{2,1,0:T(8,128)}, u32[]{:S(2)}, u32[]{:S(2)}) %collective-permute-start.32) | collective-permute-done | bytes 40992 | tf_op jit(solution)/shard_map/cond/branch_0_fun/ppermute | solution.py:189
  66.3 0.0 collective-permute-done.101.refs_7_
  66.3 2.9 %section.4 = (f32[5,16,16,128]{3,2,1,0:T(8,128)S(1)}, f32[10,16,128]{2,1,0:T(8,128)S(1)}, f32[10,16,128]{2,1,0:T(8,128)S(1)}, f32[5,16,128]{2,1,0:T(8,128)S(1)}) custom-call(s32[1]{0:T(128)} %bitcast.place.refs_0_, f32[3,5,5]{2,1,0:T(8,128)S(1)} %copy.7.refs_1_, f32[3,2,16,16]{3,2,1,0:T(8,128)S(1)} %copy-done.2, ...), custom_call_target="tpu_custom_call" | custom-call | tf_op jit(solution)/shard_map/section/pallas_call | solution.py:153
  69.2 1.9 %collective-permute-start.102 = (f32[10,16,128]{2,1,0:T(8,128)S(1)}, f32[10,16,128]{2,1,0:T(8,128)S(1)}, u32[]{:S(2)}, u32[]{:S(2)}) collective-permute-start(f32[10,16,128]{2,1,0:T(8,128)S(1)} %get-tuple-element.219), channel_id=1, source_target_pairs={{0,8},{8,16},{16,24},{24,32},{32,40},{40,48},{48,56},{56,64},{64,7... | collective-permute-start | bytes 245768 | tf_op jit(solution)/shard_map/ppermute | solution.py:203
  71.1 8.1 %collective-permute-start.103 = (f32[10,16,128]{2,1,0:T(8,128)S(1)}, f32[10,16,128]{2,1,0:T(8,128)S(1)}, u32[]{:S(2)}, u32[]{:S(2)}) collective-permute-start(f32[10,16,128]{2,1,0:T(8,128)S(1)} %get-tuple-element.220.refs_9_), channel_id=1, source_target_pairs={{0,760},{8,0},{16,8},{24,16},{32,24},{40,32},{48,40},{56,48},{64,5... | collective-permute-start | bytes 245768 | tf_op jit(solution)/shard_map/ppermute | solution.py:204
  79.9 1.9 %collective-permute-start.104 = (f32[5,16,128]{2,1,0:T(8,128)S(1)}, f32[5,16,128]{2,1,0:T(8,128)S(1)}, u32[]{:S(2)}, u32[]{:S(2)}) collective-permute-start(f32[5,16,128]{2,1,0:T(8,128)S(1)} %get-tuple-element.221), channel_id=1, source_target_pairs={{0,1},{1,0},{2,3},{3,2},{4,5},{5,4},{6,7},{7,6},{8,9},{9,8},{10,11... | collective-permute-start | bytes 122888 | tf_op jit(solution)/shard_map/ppermute | solution.py:205
  81.9 0.0 collective-permute-done.102.refs_5_
  81.9 0.0 collective-permute-done.103.refs_6_
  81.9 13.9 %conditional.5 = (f32[5,16,128]{2,1,0:T(8,128)}) conditional(s32[]{:T(128)} %clamp.11, f32[5,16,128]{2,1,0:T(8,128)S(1)} %fusion, f32[5,16,128]{2,1,0:T(8,128)S(1)} %fusion, f32[5,16,128]{2,1,0:T(8,128)S(1)} %fusion, f32[5,16,128]{2,1,0:T(8,128)S(1)} %fusion, f32[5,16,128]{2,1,0:T(8,128)S(1)} %fusion, ...), branch_computations={%region_64.65_spmd, %region_65.66_spmd, %region_66.67_spmd, %regio... | conditional | bytes 163888 | solution.py:191
  81.9 1.9 %collective-permute-start.66 = (f32[5,16,128]{2,1,0:T(8,128)S(1)}, f32[5,16,128]{2,1,0:T(8,128)}, u32[]{:S(2)}, u32[]{:S(2)}) collective-permute-start(f32[5,16,128]{2,1,0:T(8,128)S(1)} %param.66), channel_id=1, source_target_pairs={{1,2},{2,1},{9,10},{10,9},{17,18},{18,17},{25,26},{26,25},{33,34},... | collective-permute-start | bytes 122888 | tf_op jit(solution)/shard_map/cond/branch_2_fun/ppermute | solution.py:189
  83.9 11.9 %collective-permute-done.66 = f32[5,16,128]{2,1,0:T(8,128)} collective-permute-done((f32[5,16,128]{2,1,0:T(8,128)S(1)}, f32[5,16,128]{2,1,0:T(8,128)}, u32[]{:S(2)}, u32[]{:S(2)}) %collective-permute-start.66) | collective-permute-done | bytes 40992 | tf_op jit(solution)/shard_map/cond/branch_2_fun/ppermute | solution.py:189
  95.8 0.0 collective-permute-done.104.refs_7_
  95.8 3.7 %section.5 = f32[5,16,16,128]{3,2,1,0:T(8,128)} custom-call(s32[1]{0:T(128)} %bitcast.place.refs_0_, f32[3,5,5]{2,1,0:T(8,128)S(1)} %copy.7.refs_1_, f32[3,2,16,16]{3,2,1,0:T(8,128)S(1)} %copy-done.2, f32[5,16,16,128]{3,2,1,0:T(8,128)S(1)} %get-tuple-element.218.refs_3_, f32[5,16,16,128]{3,2,1,0:T(8,128)S(1)} %copy-done.1, ...), custom_call_target="tpu_custom_call" | custom-call | tf_op jit(solution)/shard_map/section/pallas_call | solution.py:153
  (4 shorter events, 0.0 us)
Async XLA Ops:
  0.0 1.1 %copy-start = (f32[5,16,16,128]{3,2,1,0:T(8,128)S(1)}, f32[5,16,16,128]{3,2,1,0:T(8,128)}, u32[]{:S(2)}) copy-start(f32[5,16,16,128]{3,2,1,0:T(8,128)} %refs_4_.5) | copy-start | bytes 1966084
  1.1 42.3 %copy-start.1 = (f32[5,16,16,128]{3,2,1,0:T(8,128)S(1)}, f32[5,16,16,128]{3,2,1,0:T(8,128)}, u32[]{:S(2)}) copy-start(f32[5,16,16,128]{3,2,1,0:T(8,128)} %refs_4_.5) | copy-start | bytes 1966084
  1.2 23.5 %collective-permute-start.97 = (f32[10,16,128]{2,1,0:T(8,128)S(1)}, f32[10,16,128]{2,1,0:T(8,128)S(1)}, u32[]{:S(2)}, u32[]{:S(2)}) collective-permute-start(f32[10,16,128]{2,1,0:T(8,128)S(1)} %get-tuple-element.212.refs_9_), channel_id=1, source_target_pairs={{0,760},{8,0},{16,8},{24,16},{32,24},{40,32},{48,40},{56,48},{64,5... | collective-permute-start | bytes 245768 | tf_op jit(solution)/shard_map/ppermute | solution.py:204
  18.9 3.9 %copy-start.4 = (s32[3]{0:T(128)S(1)}, s32[3]{0:T(128)}, u32[]{:S(2)}) copy-start(s32[3]{0:T(128)} %param.103) | copy-start | bytes 40
  18.9 10.6 %collective-permute-start.96 = (f32[10,16,128]{2,1,0:T(8,128)S(1)}, f32[10,16,128]{2,1,0:T(8,128)S(1)}, u32[]{:S(2)}, u32[]{:S(2)}) collective-permute-start(f32[10,16,128]{2,1,0:T(8,128)S(1)} %get-tuple-element.211), channel_id=1, source_target_pairs={{0,8},{8,16},{16,24},{24,32},{32,40},{40,48},{48,56},{56,64},{64,7... | collective-permute-start | bytes 245768 | tf_op jit(solution)/shard_map/ppermute | solution.py:203
  20.9 22.5 %collective-permute-start.98 = (f32[5,16,128]{2,1,0:T(8,128)S(1)}, f32[5,16,128]{2,1,0:T(8,128)S(1)}, u32[]{:S(2)}, u32[]{:S(2)}) collective-permute-start(f32[5,16,128]{2,1,0:T(8,128)S(1)} %get-tuple-element.213), channel_id=1, source_target_pairs={{0,1},{1,0},{2,3},{3,2},{4,5},{5,4},{6,7},{7,6},{8,9},{9,8},{10,11... | collective-permute-start | bytes 122888 | tf_op jit(solution)/shard_map/ppermute | solution.py:205
  24.1 0.7 copy-start.3
  29.5 13.9 %copy-start.2 = (f32[3,2,16,16]{3,2,1,0:T(8,128)S(1)}, f32[3,2,16,16]{3,2,1,0:T(8,128)}, u32[]{:S(2)}) copy-start(f32[3,2,16,16]{3,2,1,0:T(8,128)} %refs_2_.5) | copy-start | bytes 18436
  29.5 13.8 %collective-permute-start.2 = (f32[5,16,128]{2,1,0:T(8,128)S(1)}, f32[5,16,128]{2,1,0:T(8,128)}, u32[]{:S(2)}, u32[]{:S(2)}) collective-permute-start(f32[5,16,128]{2,1,0:T(8,128)S(1)} %param.2), channel_id=1, source_target_pairs={{1,2},{2,1},{9,10},{10,9},{17,18},{18,17},{25,26},{26,25},{33,34},... | collective-permute-start | bytes 122888 | tf_op jit(solution)/shard_map/cond/branch_2_fun/ppermute | solution.py:189
  46.2 8.5 %collective-permute-start.100 = (f32[10,16,128]{2,1,0:T(8,128)S(1)}, f32[10,16,128]{2,1,0:T(8,128)S(1)}, u32[]{:S(2)}, u32[]{:S(2)}) collective-permute-start(f32[10,16,128]{2,1,0:T(8,128)S(1)} %get-tuple-element.216.refs_9_), channel_id=1, source_target_pairs={{0,760},{8,0},{16,8},{24,16},{32,24},{40,32},{48,40},{56,48},{64,5... | collective-permute-start | bytes 245768 | tf_op jit(solution)/shard_map/ppermute | solution.py:204
  48.2 10.6 %collective-permute-start.99 = (f32[10,16,128]{2,1,0:T(8,128)S(1)}, f32[10,16,128]{2,1,0:T(8,128)S(1)}, u32[]{:S(2)}, u32[]{:S(2)}) collective-permute-start(f32[10,16,128]{2,1,0:T(8,128)S(1)} %get-tuple-element.215), channel_id=1, source_target_pairs={{0,8},{8,16},{16,24},{24,32},{32,40},{40,48},{48,56},{56,64},{64,7... | collective-permute-start | bytes 245768 | tf_op jit(solution)/shard_map/ppermute | solution.py:203
  52.8 13.5 %collective-permute-start.101 = (f32[5,16,128]{2,1,0:T(8,128)S(1)}, f32[5,16,128]{2,1,0:T(8,128)S(1)}, u32[]{:S(2)}, u32[]{:S(2)}) collective-permute-start(f32[5,16,128]{2,1,0:T(8,128)S(1)} %get-tuple-element.217), channel_id=1, source_target_pairs={{0,1},{1,0},{2,3},{3,2},{4,5},{5,4},{6,7},{7,6},{8,9},{9,8},{10,11... | collective-permute-start | bytes 122888 | tf_op jit(solution)/shard_map/ppermute | solution.py:205
  58.8 7.5 %collective-permute-start.32 = (f32[5,16,128]{2,1,0:T(8,128)S(1)}, f32[5,16,128]{2,1,0:T(8,128)}, u32[]{:S(2)}, u32[]{:S(2)}) collective-permute-start(f32[5,16,128]{2,1,0:T(8,128)S(1)} %param.32), channel_id=1, source_target_pairs={{1,2},{2,1},{9,10},{10,9},{17,18},{18,17},{25,26},{26,25},{33,34},... | collective-permute-start | bytes 122888 | tf_op jit(solution)/shard_map/cond/branch_0_fun/ppermute | solution.py:189
  69.2 12.7 %collective-permute-start.102 = (f32[10,16,128]{2,1,0:T(8,128)S(1)}, f32[10,16,128]{2,1,0:T(8,128)S(1)}, u32[]{:S(2)}, u32[]{:S(2)}) collective-permute-start(f32[10,16,128]{2,1,0:T(8,128)S(1)} %get-tuple-element.219), channel_id=1, source_target_pairs={{0,8},{8,16},{16,24},{24,32},{32,40},{40,48},{48,56},{56,64},{64,7... | collective-permute-start | bytes 245768 | tf_op jit(solution)/shard_map/ppermute | solution.py:203
  71.1 10.8 %collective-permute-start.103 = (f32[10,16,128]{2,1,0:T(8,128)S(1)}, f32[10,16,128]{2,1,0:T(8,128)S(1)}, u32[]{:S(2)}, u32[]{:S(2)}) collective-permute-start(f32[10,16,128]{2,1,0:T(8,128)S(1)} %get-tuple-element.220.refs_9_), channel_id=1, source_target_pairs={{0,760},{8,0},{16,8},{24,16},{32,24},{40,32},{48,40},{56,48},{64,5... | collective-permute-start | bytes 245768 | tf_op jit(solution)/shard_map/ppermute | solution.py:204
  79.9 15.8 %collective-permute-start.104 = (f32[5,16,128]{2,1,0:T(8,128)S(1)}, f32[5,16,128]{2,1,0:T(8,128)S(1)}, u32[]{:S(2)}, u32[]{:S(2)}) collective-permute-start(f32[5,16,128]{2,1,0:T(8,128)S(1)} %get-tuple-element.221), channel_id=1, source_target_pairs={{0,1},{1,0},{2,3},{3,2},{4,5},{5,4},{6,7},{7,6},{8,9},{9,8},{10,11... | collective-permute-start | bytes 122888 | tf_op jit(solution)/shard_map/ppermute | solution.py:205
  81.9 13.8 %collective-permute-start.66 = (f32[5,16,128]{2,1,0:T(8,128)S(1)}, f32[5,16,128]{2,1,0:T(8,128)}, u32[]{:S(2)}, u32[]{:S(2)}) collective-permute-start(f32[5,16,128]{2,1,0:T(8,128)S(1)} %param.66), channel_id=1, source_target_pairs={{1,2},{2,1},{9,10},{10,9},{17,18},{18,17},{25,26},{26,25},{33,34},... | collective-permute-start | bytes 122888 | tf_op jit(solution)/shard_map/cond/branch_2_fun/ppermute | solution.py:189

commit v3 on v2

--- a/solution.py
+++ b/solution.py
@@ -29,7 +29,7 @@
 
 
 def rims_kernel(place, current, low_rim, high_rim, core_rim):
-    is_odd = place[0] % 2 == 1
+    is_odd = lax.rem(place[0], 2) == 1
     cells = current.shape[1]
     for v in range(NVAR):
         low_rim[v] = current[v, 0]
@@ -47,8 +47,8 @@
     place, flux, weights, current, conserved, before, after, core_in, hop_in, hop_own = refs[:10]
     rims = refs[11:-2]
     out, low_ghost, high_ghost = refs[10], refs[-2], refs[-1]
-    index = place[0]
-    is_odd = index % 2 == 1
+    index = lax.rem(place[0], blocks)
+    is_odd = lax.rem(index, 2) == 1
     cells, width, radial = current.shape[1:]
     at_plane = (index == blocks // 2) | (index == blocks // 2 - 1)
     at_end = (index == 0) | (index == blocks - 1)
@@ -106,7 +106,7 @@
                 smooth[w] = smooth[w] + keep * conserved[w, t]
             dt, da, dr = tp - tm, ap - am, rp - rm
             for v in range(NVAR):
-                term = flux[0, v, w] * dt + flux[1, v, w] * da + flux[2, v, w] * dr
+                term = flux[v, 0, w] * dt + flux[v, 1, w] * da + flux[v, 2, w] * dr
                 slope[v] = term if slope[v] is None else slope[v] + term
         for v in range(NVAR):
             new = smooth[v] - (0.5 * push) * slope[v]
@@ -119,7 +119,7 @@
         return carry
 
     cell_row(0, lambda w: before[w], lambda w: current[w, 1])
-    lax.fori_loop(1, cells - 1, step, 0)
+    lax.fori_loop(1, cells - 1, step, 0, unroll=2)
     cell_row(cells - 1, lambda w: current[w, cells - 2], lambda w: after[w])
     if not last:
         for v in range(NVAR):
@@ -179,11 +179,15 @@
     return pairs
 
 
-def exchange_hop(own, before, after, offset, side, sectors, blocks):
-    fine = (offset + 1) % 3 - 1
-    coarse = (offset + 1) // 3 % (sectors // 3)
-    turn = fine * side
-    face = jnp.where(turn == 1, before, jnp.where(turn == -1, after, own))
+def exchange_hop(own, before, after, offset, index, sectors, blocks):
+    moved = offset + 1
+    thirds = (moved * 171) >> 9
+    coarse = jnp.where(thirds == sectors // 3, 0, thirds)
+    fine = moved - 3 * thirds
+    rotor, stator = index == blocks // 2 - 1, index == blocks // 2
+    take_before = ((fine == 2) & rotor) | ((fine == 0) & stator)
+    take_after = ((fine == 0) & rotor) | ((fine == 2) & stator)
+    face = jnp.where(take_before, before, jnp.where(take_after, after, own))
 
     def hop(by, value):
         return lax.ppermute(value, AXES, hop_pairs(by, sectors, blocks))
@@ -194,8 +198,8 @@
 def local(conserved, flux_matrices, slide_weights, rotor_offsets):
     sectors, blocks = lax.axis_size("theta"), lax.axis_size("axial")
     index = lax.axis_index("axial")
-    place = jnp.full((1,), index, jnp.int32)
-    side = jnp.where(index == blocks // 2 - 1, 1, jnp.where(index == blocks // 2, -1, 0))
+    place = jnp.full((1,), lax.axis_index("theta") * blocks + index, jnp.int32)
+    flux = jnp.transpose(flux_matrices, (1, 0, 2))
     current, rims = conserved, first_rims(place, conserved)
     sections = len(SECTION_WEIGHTS)
     for section in range(sections):
@@ -208,7 +212,7 @@
             before[NVAR:],
             after[NVAR:],
             rotor_offsets[section],
-            side,
+            index,
             sectors,
             blocks,
         )
@@ -217,7 +221,7 @@
             blocks,
             section == sections - 1,
             place,
-            flux_matrices,
+            flux,
             slide_weights,
             current,
             conserved,

time: 100 us -> 94.2 us (0.942)
  the two profiles are of different devices: /device:TPU:40 before, /device:TPU:32 now
where the time goes in v3:
time: 94.2 us; the launch traced here: 93.5 us
  starting transfers between devices  54.4 us (58%)
  waiting for transfers between devices  26.4 us (28%)
  Pallas kernels  8.11 us (9%)
  local copies, waits for them, and re-layouts  2.4 us (3%)
  between operations  2.11 us (2%)
    ppermute x3, starting transfers between devices, local(): after = lax.ppermute(low_rim, 'theta', ring(-1, sectors))  35.5 us
    ppermute x3, waiting for transfers between devices, hop(): return lax.ppermute(value, AXES, hop_pairs(by, sectors, blocks))  25.9 us
    pallas_call x3, Pallas kernels, advance(): pl.pallas_call(functools.partial(section_kernel, section, blocks, last),...  7.98 us
    ppermute x3, starting transfers between devices, local(): before = lax.ppermute(high_rim, 'theta', ring(1, sectors))  7.24 us
    ppermute x3, starting transfers between devices, local(): core_in = lax.ppermute(core_rim, 'axial', core_pairs(blocks))  5.89 us
    ppermute x3, starting transfers between devices, hop(): return lax.ppermute(value, AXES, hop_pairs(by, sectors, blocks))  5.76 us
  transfers between devices with their start and end apart: 12, of which 4 were waited for; matrix products, arithmetic and copies ran while one was open for 1% of the time, Pallas kernels for 0%

profile of v3, /device:TPU:32, one launch (start us, length us, event | category | flops | bytes accessed | tf_op | source)
XLA Modules:
  0.0 93.5 jit_solution(12246186409527459941)
XLA Ops:
  0.0 0.0 copy-start
  0.0 1.1 %copy-done = f32[5,16,16,128]{3,2,1,0:T(8,128)S(1)} copy-done((f32[5,16,16,128]{3,2,1,0:T(8,128)S(1)}, f32[5,16,16,128]{3,2,1,0:T(8,128)}, u32[]{:S(2)}) %copy-start) | copy-done | bytes 655384
  1.1 0.0 copy-start.1
  1.1 0.1 rims.1
  1.2 2.1 %collective-permute-start.98 = (f32[5,16,128]{2,1,0:T(8,128)S(1)}, f32[5,16,128]{2,1,0:T(8,128)S(1)}, u32[]{:S(2)}, u32[]{:S(2)}) collective-permute-start(f32[5,16,128]{2,1,0:T(8,128)S(1)} %get-tuple-element.213), channel_id=1, source_target_pairs={{0,1},{1,0},{2,3},{3,2},{4,5},{5,4},{6,7},{7,6},{8,9},{9,8},{10,11... | collective-permute-start | bytes 122888 | tf_op jit(solution)/shard_map/ppermute | solution.py:209
  3.3 3.4 %collective-permute-start.96 = (f32[10,16,128]{2,1,0:T(8,128)S(1)}, f32[10,16,128]{2,1,0:T(8,128)S(1)}, u32[]{:S(2)}, u32[]{:S(2)}) collective-permute-start(f32[10,16,128]{2,1,0:T(8,128)S(1)} %get-tuple-element.211), channel_id=1, source_target_pairs={{0,8},{8,16},{16,24},{24,32},{32,40},{40,48},{48,56},{56,64},{64,7... | collective-permute-start | bytes 245768 | tf_op jit(solution)/shard_map/ppermute | solution.py:207
  6.7 15.4 %collective-permute-start.97 = (f32[10,16,128]{2,1,0:T(8,128)S(1)}, f32[10,16,128]{2,1,0:T(8,128)S(1)}, u32[]{:S(2)}, u32[]{:S(2)}) collective-permute-start(f32[10,16,128]{2,1,0:T(8,128)S(1)} %get-tuple-element.212.refs_9_), channel_id=1, source_target_pairs={{0,760},{8,0},{16,8},{24,16},{32,24},{40,32},{48,40},{56,48},{64,5... | collective-permute-start | bytes 245768 | tf_op jit(solution)/shard_map/ppermute | solution.py:208
  22.1 0.0 copy-start.4
  22.1 0.6 copy-done.4
  22.8 0.6 fusion.3
  24.0 0.0 collective-permute-done.96.refs_5_
  24.0 0.4 collective-permute-done.97.refs_6_
  24.5 0.0 copy-start.2
  24.5 0.0 copy-start.3
  24.5 9.8 %conditional.3 = (f32[5,16,128]{2,1,0:T(8,128)}) conditional(s32[]{:T(128)} %clamp.9, f32[5,16,128]{2,1,0:T(8,128)S(1)} %fusion.2, f32[5,16,128]{2,1,0:T(8,128)S(1)} %fusion.2, f32[5,16,128]{2,1,0:T(8,128)S(1)} %fusion.2, f32[5,16,128]{2,1,0:T(8,128)S(1)} %fusion.2, f32[5,16,128]{2,1,0:T(8,128)S(1)} %fusion.2, ...), branch_computations={%region_0.1_spmd, %region_1.2_spmd, %region_2.3_spmd, %region_3.4_... | conditional | bytes 163888 | solution.py:195
  24.5 1.9 %collective-permute-start.31 = (f32[5,16,128]{2,1,0:T(8,128)S(1)}, f32[5,16,128]{2,1,0:T(8,128)}, u32[]{:S(2)}, u32[]{:S(2)}) collective-permute-start(f32[5,16,128]{2,1,0:T(8,128)S(1)} %param.31), channel_id=1, source_target_pairs={{1,2},{2,1},{9,10},{10,9},{17,18},{18,17},{25,26},{26,25},{33,34},... | collective-permute-start | bytes 122888 | tf_op jit(solution)/shard_map/cond/branch_31_fun/ppermute | solution.py:193
  26.5 7.8 %collective-permute-done.31 = f32[5,16,128]{2,1,0:T(8,128)} collective-permute-done((f32[5,16,128]{2,1,0:T(8,128)S(1)}, f32[5,16,128]{2,1,0:T(8,128)}, u32[]{:S(2)}, u32[]{:S(2)}) %collective-permute-start.31) | collective-permute-done | bytes 40992 | tf_op jit(solution)/shard_map/cond/branch_31_fun/ppermute | solution.py:193
  34.3 0.0 collective-permute-done.98.refs_7_
  34.3 0.0 copy-done.1
  34.3 0.0 copy-done.2
  34.3 0.0 copy-done.3
  34.3 2.4 %section.3 = (f32[5,16,16,128]{3,2,1,0:T(8,128)S(1)}, f32[10,16,128]{2,1,0:T(8,128)S(1)}, f32[10,16,128]{2,1,0:T(8,128)S(1)}, f32[5,16,128]{2,1,0:T(8,128)S(1)}) custom-call(s32[1]{0:T(128)} %bitcast.place.refs_0_, f32[5,3,5]{2,1,0:T(4,128)S(1)} %bitcast.5, f32[3,2,16,16]{3,2,1,0:T(8,128)S(1)} %copy-done.2, f32[5,16,16,128]{3,2,1,0:T(8,128)S(1)} %copy-done.1, ...), custom_call_target="tpu_custom_call" | custom-call | tf_op jit(solution)/shard_map/section/pallas_call | solution.py:153
  36.7 1.9 %collective-permute-start.99 = (f32[10,16,128]{2,1,0:T(8,128)S(1)}, f32[10,16,128]{2,1,0:T(8,128)S(1)}, u32[]{:S(2)}, u32[]{:S(2)}) collective-permute-start(f32[10,16,128]{2,1,0:T(8,128)S(1)} %get-tuple-element.215), channel_id=1, source_target_pairs={{0,8},{8,16},{16,24},{24,32},{32,40},{40,48},{48,56},{56,64},{64,7... | collective-permute-start | bytes 245768 | tf_op jit(solution)/shard_map/ppermute | solution.py:207
  38.6 10.3 %collective-permute-start.100 = (f32[10,16,128]{2,1,0:T(8,128)S(1)}, f32[10,16,128]{2,1,0:T(8,128)S(1)}, u32[]{:S(2)}, u32[]{:S(2)}) collective-permute-start(f32[10,16,128]{2,1,0:T(8,128)S(1)} %get-tuple-element.216.refs_9_), channel_id=1, source_target_pairs={{0,760},{8,0},{16,8},{24,16},{32,24},{40,32},{48,40},{56,48},{64,5... | collective-permute-start | bytes 245768 | tf_op jit(solution)/shard_map/ppermute | solution.py:208
  49.6 1.9 %collective-permute-start.101 = (f32[5,16,128]{2,1,0:T(8,128)S(1)}, f32[5,16,128]{2,1,0:T(8,128)S(1)}, u32[]{:S(2)}, u32[]{:S(2)}) collective-permute-start(f32[5,16,128]{2,1,0:T(8,128)S(1)} %get-tuple-element.217), channel_id=1, source_target_pairs={{0,1},{1,0},{2,3},{3,2},{4,5},{5,4},{6,7},{7,6},{8,9},{9,8},{10,11... | collective-permute-start | bytes 122888 | tf_op jit(solution)/shard_map/ppermute | solution.py:209
  51.5 0.0 collective-permute-done.99.refs_5_
  51.5 0.0 collective-permute-done.100.refs_6_
  51.5 12.4 %conditional.4 = (f32[5,16,128]{2,1,0:T(8,128)}) conditional(s32[]{:T(128)} %clamp.10, f32[5,16,128]{2,1,0:T(8,128)S(1)} %fusion.1, f32[5,16,128]{2,1,0:T(8,128)S(1)} %fusion.1, f32[5,16,128]{2,1,0:T(8,128)S(1)} %fusion.1, f32[5,16,128]{2,1,0:T(8,128)S(1)} %fusion.1, f32[5,16,128]{2,1,0:T(8,128)S(1)} %fusion.1, ...), branch_computations={%region_32.33_spmd, %region_33.34_spmd, %region_34.35_spmd, %regio... | conditional | bytes 163888 | solution.py:195
  51.6 1.9 %collective-permute-start.59 = (f32[5,16,128]{2,1,0:T(8,128)S(1)}, f32[5,16,128]{2,1,0:T(8,128)}, u32[]{:S(2)}, u32[]{:S(2)}) collective-permute-start(f32[5,16,128]{2,1,0:T(8,128)S(1)} %param.59), channel_id=1, source_target_pairs={{1,2},{2,1},{9,10},{10,9},{17,18},{18,17},{25,26},{26,25},{33,34},... | collective-permute-start | bytes 122888 | tf_op jit(solution)/shard_map/cond/branch_27_fun/ppermute | solution.py:193
  53.5 10.4 %collective-permute-done.59 = f32[5,16,128]{2,1,0:T(8,128)} collective-permute-done((f32[5,16,128]{2,1,0:T(8,128)S(1)}, f32[5,16,128]{2,1,0:T(8,128)}, u32[]{:S(2)}, u32[]{:S(2)}) %collective-permute-start.59) | collective-permute-done | bytes 40992 | tf_op jit(solution)/shard_map/cond/branch_27_fun/ppermute | solution.py:193
  63.9 0.0 collective-permute-done.101.refs_7_
  63.9 2.4 %section.4 = (f32[5,16,16,128]{3,2,1,0:T(8,128)S(1)}, f32[10,16,128]{2,1,0:T(8,128)S(1)}, f32[10,16,128]{2,1,0:T(8,128)S(1)}, f32[5,16,128]{2,1,0:T(8,128)S(1)}) custom-call(s32[1]{0:T(128)} %bitcast.place.refs_0_, f32[5,3,5]{2,1,0:T(4,128)S(1)} %bitcast.6, f32[3,2,16,16]{3,2,1,0:T(8,128)S(1)} %copy-done.2, ...), custom_call_target="tpu_custom_call" | custom-call | tf_op jit(solution)/shard_map/section/pallas_call | solution.py:153
  66.3 1.9 %collective-permute-start.102 = (f32[10,16,128]{2,1,0:T(8,128)S(1)}, f32[10,16,128]{2,1,0:T(8,128)S(1)}, u32[]{:S(2)}, u32[]{:S(2)}) collective-permute-start(f32[10,16,128]{2,1,0:T(8,128)S(1)} %get-tuple-element.219), channel_id=1, source_target_pairs={{0,8},{8,16},{16,24},{24,32},{32,40},{40,48},{48,56},{56,64},{64,7... | collective-permute-start | bytes 245768 | tf_op jit(solution)/shard_map/ppermute | solution.py:207
  68.3 9.7 %collective-permute-start.103 = (f32[10,16,128]{2,1,0:T(8,128)S(1)}, f32[10,16,128]{2,1,0:T(8,128)S(1)}, u32[]{:S(2)}, u32[]{:S(2)}) collective-permute-start(f32[10,16,128]{2,1,0:T(8,128)S(1)} %get-tuple-element.220.refs_9_), channel_id=1, source_target_pairs={{0,760},{8,0},{16,8},{24,16},{32,24},{40,32},{48,40},{56,48},{64,5... | collective-permute-start | bytes 245768 | tf_op jit(solution)/shard_map/ppermute | solution.py:208
  78.7 1.9 %collective-permute-start.104 = (f32[5,16,128]{2,1,0:T(8,128)S(1)}, f32[5,16,128]{2,1,0:T(8,128)S(1)}, u32[]{:S(2)}, u32[]{:S(2)}) collective-permute-start(f32[5,16,128]{2,1,0:T(8,128)S(1)} %get-tuple-element.221), channel_id=1, source_target_pairs={{0,1},{1,0},{2,3},{3,2},{4,5},{5,4},{6,7},{7,6},{8,9},{9,8},{10,11... | collective-permute-start | bytes 122888 | tf_op jit(solution)/shard_map/ppermute | solution.py:209
  80.6 0.0 collective-permute-done.102.refs_5_
  80.6 0.0 collective-permute-done.103.refs_6_
  80.7 9.7 %conditional.5 = (f32[5,16,128]{2,1,0:T(8,128)}) conditional(s32[]{:T(128)} %clamp.11, f32[5,16,128]{2,1,0:T(8,128)S(1)} %fusion, f32[5,16,128]{2,1,0:T(8,128)S(1)} %fusion, f32[5,16,128]{2,1,0:T(8,128)S(1)} %fusion, f32[5,16,128]{2,1,0:T(8,128)S(1)} %fusion, f32[5,16,128]{2,1,0:T(8,128)S(1)} %fusion, ...), branch_computations={%region_64.65_spmd, %region_65.66_spmd, %region_66.67_spmd, %regio... | conditional | bytes 163888 | solution.py:195
  80.7 1.9 %collective-permute-start.65 = (f32[5,16,128]{2,1,0:T(8,128)S(1)}, f32[5,16,128]{2,1,0:T(8,128)}, u32[]{:S(2)}, u32[]{:S(2)}) collective-permute-start(f32[5,16,128]{2,1,0:T(8,128)S(1)} %param.65), channel_id=1, source_target_pairs={{1,2},{2,1},{9,10},{10,9},{17,18},{18,17},{25,26},{26,25},{33,34},... | collective-permute-start | bytes 122888 | tf_op jit(solution)/shard_map/cond/branch_1_fun/ppermute | solution.py:193
  82.6 7.7 %collective-permute-done.65 = f32[5,16,128]{2,1,0:T(8,128)} collective-permute-done((f32[5,16,128]{2,1,0:T(8,128)S(1)}, f32[5,16,128]{2,1,0:T(8,128)}, u32[]{:S(2)}, u32[]{:S(2)}) %collective-permute-start.65) | collective-permute-done | bytes 40992 | tf_op jit(solution)/shard_map/cond/branch_1_fun/ppermute | solution.py:193
  90.3 0.0 collective-permute-done.104.refs_7_
  90.3 3.2 %section.5 = f32[5,16,16,128]{3,2,1,0:T(8,128)} custom-call(s32[1]{0:T(128)} %bitcast.place.refs_0_, f32[5,3,5]{2,1,0:T(4,128)S(1)} %bitcast.7, f32[3,2,16,16]{3,2,1,0:T(8,128)S(1)} %copy-done.2, f32[5,16,16,128]{3,2,1,0:T(8,128)S(1)} %get-tuple-element.218.refs_3_, f32[5,16,16,128]{3,2,1,0:T(8,128)S(1)} %copy-done.1, ...), custom_call_target="tpu_custom_call" | custom-call | tf_op jit(solution)/shard_map/section/pallas_call | solution.py:153
  (3 shorter events, 0.0 us)
Async XLA Ops:
  0.0 1.1 %copy-start = (f32[5,16,16,128]{3,2,1,0:T(8,128)S(1)}, f32[5,16,16,128]{3,2,1,0:T(8,128)}, u32[]{:S(2)}) copy-start(f32[5,16,16,128]{3,2,1,0:T(8,128)} %refs_4_.5) | copy-start | bytes 1966084
  1.1 33.2 %copy-start.1 = (f32[5,16,16,128]{3,2,1,0:T(8,128)S(1)}, f32[5,16,16,128]{3,2,1,0:T(8,128)}, u32[]{:S(2)}) copy-start(f32[5,16,16,128]{3,2,1,0:T(8,128)} %refs_4_.5) | copy-start | bytes 1966084
  1.2 33.1 %collective-permute-start.98 = (f32[5,16,128]{2,1,0:T(8,128)S(1)}, f32[5,16,128]{2,1,0:T(8,128)S(1)}, u32[]{:S(2)}, u32[]{:S(2)}) collective-permute-start(f32[5,16,128]{2,1,0:T(8,128)S(1)} %get-tuple-element.213), channel_id=1, source_target_pairs={{0,1},{1,0},{2,3},{3,2},{4,5},{5,4},{6,7},{7,6},{8,9},{9,8},{10,11... | collective-permute-start | bytes 122888 | tf_op jit(solution)/shard_map/ppermute | solution.py:209
  3.3 20.7 %collective-permute-start.96 = (f32[10,16,128]{2,1,0:T(8,128)S(1)}, f32[10,16,128]{2,1,0:T(8,128)S(1)}, u32[]{:S(2)}, u32[]{:S(2)}) collective-permute-start(f32[10,16,128]{2,1,0:T(8,128)S(1)} %get-tuple-element.211), channel_id=1, source_target_pairs={{0,8},{8,16},{16,24},{24,32},{32,40},{40,48},{48,56},{56,64},{64,7... | collective-permute-start | bytes 245768 | tf_op jit(solution)/shard_map/ppermute | solution.py:207
  6.7 17.8 %collective-permute-start.97 = (f32[10,16,128]{2,1,0:T(8,128)S(1)}, f32[10,16,128]{2,1,0:T(8,128)S(1)}, u32[]{:S(2)}, u32[]{:S(2)}) collective-permute-start(f32[10,16,128]{2,1,0:T(8,128)S(1)} %get-tuple-element.212.refs_9_), channel_id=1, source_target_pairs={{0,760},{8,0},{16,8},{24,16},{32,24},{40,32},{48,40},{56,48},{64,5... | collective-permute-start | bytes 245768 | tf_op jit(solution)/shard_map/ppermute | solution.py:208
  22.1 0.7 copy-start.4
  24.5 9.8 %copy-start.2 = (f32[3,2,16,16]{3,2,1,0:T(8,128)S(1)}, f32[3,2,16,16]{3,2,1,0:T(8,128)}, u32[]{:S(2)}) copy-start(f32[3,2,16,16]{3,2,1,0:T(8,128)} %refs_2_.5) | copy-start | bytes 18436
  24.5 9.8 %copy-start.3 = (f32[3,5,5]{2,0,1:T(4,128)S(1)}, f32[3,5,5]{2,0,1:T(4,128)}, u32[]{:S(2)}) copy-start(f32[3,5,5]{2,0,1:T(4,128)} %param.101) | copy-start | bytes 904
  24.5 9.7 %collective-permute-start.31 = (f32[5,16,128]{2,1,0:T(8,128)S(1)}, f32[5,16,128]{2,1,0:T(8,128)}, u32[]{:S(2)}, u32[]{:S(2)}) collective-permute-start(f32[5,16,128]{2,1,0:T(8,128)S(1)} %param.31), channel_id=1, source_target_pairs={{1,2},{2,1},{9,10},{10,9},{17,18},{18,17},{25,26},{26,25},{33,34},... | collective-permute-start | bytes 122888 | tf_op jit(solution)/shard_map/cond/branch_31_fun/ppermute | solution.py:193
  36.7 14.8 %collective-permute-start.99 = (f32[10,16,128]{2,1,0:T(8,128)S(1)}, f32[10,16,128]{2,1,0:T(8,128)S(1)}, u32[]{:S(2)}, u32[]{:S(2)}) collective-permute-start(f32[10,16,128]{2,1,0:T(8,128)S(1)} %get-tuple-element.215), channel_id=1, source_target_pairs={{0,8},{8,16},{16,24},{24,32},{32,40},{40,48},{48,56},{56,64},{64,7... | collective-permute-start | bytes 245768 | tf_op jit(solution)/shard_map/ppermute | solution.py:207
  38.6 12.9 %collective-permute-start.100 = (f32[10,16,128]{2,1,0:T(8,128)S(1)}, f32[10,16,128]{2,1,0:T(8,128)S(1)}, u32[]{:S(2)}, u32[]{:S(2)}) collective-permute-start(f32[10,16,128]{2,1,0:T(8,128)S(1)} %get-tuple-element.216.refs_9_), channel_id=1, source_target_pairs={{0,760},{8,0},{16,8},{24,16},{32,24},{40,32},{48,40},{56,48},{64,5... | collective-permute-start | bytes 245768 | tf_op jit(solution)/shard_map/ppermute | solution.py:208
  49.6 14.4 %collective-permute-start.101 = (f32[5,16,128]{2,1,0:T(8,128)S(1)}, f32[5,16,128]{2,1,0:T(8,128)S(1)}, u32[]{:S(2)}, u32[]{:S(2)}) collective-permute-start(f32[5,16,128]{2,1,0:T(8,128)S(1)} %get-tuple-element.217), channel_id=1, source_target_pairs={{0,1},{1,0},{2,3},{3,2},{4,5},{5,4},{6,7},{7,6},{8,9},{9,8},{10,11... | collective-permute-start | bytes 122888 | tf_op jit(solution)/shard_map/ppermute | solution.py:209
  51.6 12.3 %collective-permute-start.59 = (f32[5,16,128]{2,1,0:T(8,128)S(1)}, f32[5,16,128]{2,1,0:T(8,128)}, u32[]{:S(2)}, u32[]{:S(2)}) collective-permute-start(f32[5,16,128]{2,1,0:T(8,128)S(1)} %param.59), channel_id=1, source_target_pairs={{1,2},{2,1},{9,10},{10,9},{17,18},{18,17},{25,26},{26,25},{33,34},... | collective-permute-start | bytes 122888 | tf_op jit(solution)/shard_map/cond/branch_27_fun/ppermute | solution.py:193
  66.3 14.3 %collective-permute-start.102 = (f32[10,16,128]{2,1,0:T(8,128)S(1)}, f32[10,16,128]{2,1,0:T(8,128)S(1)}, u32[]{:S(2)}, u32[]{:S(2)}) collective-permute-start(f32[10,16,128]{2,1,0:T(8,128)S(1)} %get-tuple-element.219), channel_id=1, source_target_pairs={{0,8},{8,16},{16,24},{24,32},{32,40},{40,48},{48,56},{56,64},{64,7... | collective-permute-start | bytes 245768 | tf_op jit(solution)/shard_map/ppermute | solution.py:207
  68.3 12.4 %collective-permute-start.103 = (f32[10,16,128]{2,1,0:T(8,128)S(1)}, f32[10,16,128]{2,1,0:T(8,128)S(1)}, u32[]{:S(2)}, u32[]{:S(2)}) collective-permute-start(f32[10,16,128]{2,1,0:T(8,128)S(1)} %get-tuple-element.220.refs_9_), channel_id=1, source_target_pairs={{0,760},{8,0},{16,8},{24,16},{32,24},{40,32},{48,40},{56,48},{64,5... | collective-permute-start | bytes 245768 | tf_op jit(solution)/shard_map/ppermute | solution.py:208
  78.7 11.6 %collective-permute-start.104 = (f32[5,16,128]{2,1,0:T(8,128)S(1)}, f32[5,16,128]{2,1,0:T(8,128)S(1)}, u32[]{:S(2)}, u32[]{:S(2)}) collective-permute-start(f32[5,16,128]{2,1,0:T(8,128)S(1)} %get-tuple-element.221), channel_id=1, source_target_pairs={{0,1},{1,0},{2,3},{3,2},{4,5},{5,4},{6,7},{7,6},{8,9},{9,8},{10,11... | collective-permute-start | bytes 122888 | tf_op jit(solution)/shard_map/ppermute | solution.py:209
  80.7 9.6 %collective-permute-start.65 = (f32[5,16,128]{2,1,0:T(8,128)S(1)}, f32[5,16,128]{2,1,0:T(8,128)}, u32[]{:S(2)}, u32[]{:S(2)}) collective-permute-start(f32[5,16,128]{2,1,0:T(8,128)S(1)} %param.65), channel_id=1, source_target_pairs={{1,2},{2,1},{9,10},{10,9},{17,18},{18,17},{25,26},{26,25},{33,34},... | collective-permute-start | bytes 122888 | tf_op jit(solution)/shard_map/cond/branch_1_fun/ppermute | solution.py:193
